TPU v7x, 128 devices: a whole 4x4x4 slice. The times are simulated.
128 devices in a mesh: gx: 16 (over x, y), gy: 8 (over z, core).
Axes of the slice: x: 4, y: 4, z: 4, core: 2. Of those that a mesh axis runs over, the one named last changes fastest.
Arguments:
- thermal_deviation: float32 [2048, 512, 128], P('gx', 'gy'), may hold values from -6 to 6
- darcy_flux: bfloat16 [3, 2048, 512, 128], P(None, 'gx', 'gy'), may hold values from -1 to 1
- mixing_coefficient: bfloat16 [2, 2048, 512, 128], P(None, 'gx', 'gy'), may hold values from 0.049804688 to 0.59765625
- well_patch_site: int32 [16, 8, 128, 8], P('gx', 'gy'), may hold values from 0 to 8191, as said below
- well_stratum_first: int32 [16, 8, 128, 8], P('gx', 'gy'), may hold values from 0 to 31, as said below
- well_stratum_stop: int32 [16, 8, 128, 8], P('gx', 'gy'), may hold values from 0 to 95, as said below
- arriving_entry_lookup: int32 [16, 8, 1024], P('gx', 'gy'), may hold values from 0 to 1024, as said below
- arrived_circuit_order: int32 [16, 8, 1024], P('gx', 'gy'), may hold values from 0 to 1024, as said below
- circuit_solver_operator: float32 [16, 8, 32, 32, 32], P('gx', 'gy')
Outputs:
- new_temperature: float32 [2048, 512, 128], P('gx', 'gy')
- heat_rates: float32 [16, 8, 1024, 128], P('gx', 'gy')
Inputs may be any that keep to these rules, and one draw needn't show every extreme that they name: `well_patch_site`: A cell within one tile. A slot is live when well_stratum_stop > well_stratum_first; dead slots have both 0. For each tile and owner the live slots are slots 0 to n - 1 with n from 1 to 8; n is 8 for a tile's own owner index. Live boreholes span 128 // 4 to 64 layers starting above layer 32. `well_stratum_stop`: see well_stratum_first. `arriving_entry_lookup`: each live received slot fills exactly one loop position; unfilled positions hold 1024. `arrived_circuit_order`: the inverse of arriving_entry_lookup on live slots; dead received slots hold 1024.
All inputs are finite; a program needn't handle non-finite values.
Results may differ from a plain program's by a relative error of at most 0.0003.
Values sent between devices are 32-bit elements; how exact they have to be, the bound alone decides.
A program may use at most 192 MiB of HBM per device.

v0:
```python
import jax
import jax.numpy as jnp
from jax import lax
from jax.sharding import PartitionSpec as P

STEPS = 2


def extended_2(x, sides, width):
    for axis, dim in sides:
        devices, length = (lax.axis_size(axis), x.shape[dim])
        up = [(i, (i + 1) % devices) for i in range(devices - 1)]
        down = [(j, i) for i, j in up]
        last = lax.slice_in_dim(x, length - width, length, axis=dim)
        initial = lax.slice_in_dim(x, 0, width, axis=dim)
        before = lax.ppermute(last, axis, up)
        after = lax.ppermute(initial, axis, down)
        x = jnp.concatenate([before, x, after], axis=dim)
    return x


def tendency(padded, darcy_flux, mixing_coefficient):
    full = jnp.pad(padded, ((0, 0), (0, 0), (1, 1)))
    centre = full[1:-1, 1:-1, 1:-1]
    x_minus = full[:-2, 1:-1, 1:-1]
    x_plus = full[2:, 1:-1, 1:-1]
    y_minus = full[1:-1, :-2, 1:-1]
    y_plus = full[1:-1, 2:, 1:-1]
    z_minus = full[1:-1, 1:-1, :-2]
    z_plus = full[1:-1, 1:-1, 2:]
    speed = darcy_flux.astype(jnp.float32)
    coeff = mixing_coefficient.astype(jnp.float32)
    advect = jnp.maximum(speed[0], 0.0) * (centre - x_minus) + jnp.minimum(speed[0], 0.0) * (
        x_plus - centre
    )
    advect = (
        advect
        + jnp.maximum(speed[1], 0.0) * (centre - y_minus)
        + jnp.minimum(speed[1], 0.0) * (y_plus - centre)
    )
    advect = (
        advect
        + jnp.maximum(speed[2], 0.0) * (centre - z_minus)
        + jnp.minimum(speed[2], 0.0) * (z_plus - centre)
    )
    spread = coeff[0] * (x_plus + x_minus + y_plus + y_minus - 4.0 * centre) + coeff[1] * (
        z_plus + z_minus - 2.0 * centre
    )
    return 0.1 * (spread - advect)


def send_columns(block):
    return lax.all_to_all(block, ("gx", "gy"), split_axis=0, concat_axis=0, tiled=True)


def send_rates(block):
    return lax.all_to_all(block, ("gx", "gy"), split_axis=0, concat_axis=0, tiled=True)


def local(
    thermal_deviation,
    darcy_flux,
    mixing_coefficient,
    well_patch_site,
    well_stratum_first,
    well_stratum_stop,
    arriving_entry_lookup,
    arrived_circuit_order,
    circuit_solver_operator,
):
    across = lax.axis_size("gx")
    along = lax.axis_size("gy")
    groups = across * along
    patch_extent_east, patch_extent_north, stratum_thickness = thermal_deviation.shape
    slots = well_patch_site.shape[-1]
    cells = well_patch_site.reshape(-1)
    own_top = well_stratum_first.reshape(-1)
    layers = jnp.arange(stratum_thickness, dtype=jnp.int32)
    masks = (
        (layers[None, :] >= own_top[:, None])
        & (layers[None, :] < well_stratum_stop.reshape(-1)[:, None])
    ).astype(jnp.float32)
    gather_index = arriving_entry_lookup.reshape(-1)
    return_index = arrived_circuit_order.reshape(-1)
    inverse = circuit_solver_operator[0, 0]
    loops_count, loop_size = (inverse.shape[0], inverse.shape[1])
    thermal_state = thermal_deviation
    rates = None
    for step in range(STEPS):
        padded = extended_2(thermal_state, (("gx", 0), ("gy", 1)), 1)
        rate = tendency(padded, darcy_flux, mixing_coefficient)
        flat_field = thermal_state.reshape(
            patch_extent_east * patch_extent_north, stratum_thickness
        )
        columns = flat_field[cells] * masks
        received = send_columns(columns.reshape(groups, slots, stratum_thickness)).reshape(
            groups * slots, stratum_thickness
        )
        received = jnp.concatenate(
            [received, jnp.zeros((1, stratum_thickness), jnp.float32)], axis=0
        )
        loops = received[gather_index].reshape(loops_count, loop_size, stratum_thickness)
        rates = jnp.einsum("bjk,bkz->bjz", inverse, loops, precision=lax.Precision.HIGHEST)
        rates = rates.reshape(loops_count * loop_size, stratum_thickness)
        extended = jnp.concatenate([rates, jnp.zeros((1, stratum_thickness), jnp.float32)], axis=0)
        outgoing = extended[return_index]
        back = (
            send_rates(outgoing.reshape(groups, slots, stratum_thickness)).reshape(
                groups * slots, stratum_thickness
            )
            * masks
        )
        deposit = (
            jnp.zeros((patch_extent_east * patch_extent_north, stratum_thickness), jnp.float32)
            .at[cells]
            .add(back)
        )
        thermal_state = (
            thermal_state
            + rate
            - deposit.reshape(patch_extent_east, patch_extent_north, stratum_thickness)
        )
    return (thermal_state, rates.reshape(1, 1, loops_count * loop_size, stratum_thickness))


def solution(mesh):
    placed = (
        P("gx", "gy", None),
        P(None, "gx", "gy", None),
        P(None, "gx", "gy", None),
        P("gx", "gy", None, None),
        P("gx", "gy", None, None),
        P("gx", "gy", None, None),
        P("gx", "gy", None),
        P("gx", "gy", None),
        P("gx", "gy", None, None, None),
    )
    return jax.shard_map(
        local,
        mesh=mesh,
        in_specs=placed,
        out_specs=(P("gx", "gy", None), P("gx", "gy", None, None)),
        check_vma=False,
    )
```

profile of v0, /device:TPU:1, one launch (start us, length us, event | category | flops | bytes accessed | tf_op | source)
XLA Modules:
  0.0 216.2 jit_solution(4266051375948520033)
XLA Ops:
  2.8 4.7 %collective-permute-start.1 = (f32[1,64,128]{2,1,0:T(8,128)S(1)}, f32[1,64,128]{2,1,0:T(8,128)S(1)}, u32[]{:S(2)}, u32[]{:S(2)}) collective-permute-start(f32[1,64,128]{2,1,0:T(8,128)S(1)} %get-tuple-element.11), channel_id=1, source_target_pairs={{0,8},{8,16},{16,24},{24,32},{32,40},{40,48},{48,56},{56,64},{64,7... | collective-permute-start | bytes 98312 | tf_op jit(solution)/shard_map/ppermute | solution.py:16
  10.0 5.0 %gather_fusion = f32[1024,128]{1,0:T(8,128)S(1)} fusion(f32[8192,128]{1,0:T(8,128)} %bitcast.93, s32[1024]{0:T(1024)S(1)} %broadcast_clamp_fusion.2), kind=kCustom, calls=%fused_computation | custom fusion | bytes 1052672 | tf_op jit(solution)/shard_map/gather | solution.py:95
  16.1 13.3 %all-to-all-start = ((f32[128,8,128]{2,1,0:T(8,128)}), f32[128,8,128]{2,1,0:T(8,128)S(1)}, u32[]{:S(2)}, u32[]{:S(2)}) async-start(f32[128,8,128]{2,1,0:T(8,128)} %bitcast_select_fusion.5), calls=%async_computation | async-start | bytes 1048576 | tf_op jit(solution)/shard_map/all_to_all | solution.py:53
  29.9 6.8 %convert_element_type.12 = f32[2,128,64,128]{3,2,1,0:T(8,128)} convert(bf16[2,128,64,128]{3,2,1,0:T(8,128)(2,1)} %param.11) | non-fusion elementwise | flops 2097152 | bytes 12582912 | tf_op jit(solution)/shard_map/convert_element_type | solution.py:32
  36.7 6.1 %convert_element_type.13 = f32[3,128,64,128]{3,2,1,0:T(8,128)} convert(bf16[3,128,64,128]{3,2,1,0:T(8,128)(2,1)S(1)} %bitcast.97) | non-fusion elementwise | flops 3145728 | bytes 18874368 | tf_op jit(solution)/shard_map/convert_element_type | solution.py:31
  45.2 3.7 %collective-permute-start.3 = (f32[130,1,128]{2,1,0:T(1,128)S(1)}, f32[130,1,128]{2,1,0:T(1,128)S(1)}, u32[]{:S(2)}, u32[]{:S(2)}) collective-permute-start(f32[130,1,128]{2,1,0:T(1,128)S(1)} %get-tuple-element.6), channel_id=1, source_target_pairs={{0,1},{1,2},{2,3},{3,4},{4,5},{5,6},{6,7},{8,9},{9,10},{10,11},{11... | collective-permute-start | bytes 199688 | tf_op jit(solution)/shard_map/ppermute | solution.py:16
  50.9 2.8 %gather_fusion.1 = f32[1024,128]{1,0:T(8,128)S(1)} fusion(f32[1025,128]{1,0:T(8,128)S(1)} %concatenate.54, s32[1024]{0:T(1024)S(1)} %broadcast_clamp_fusion.1), kind=kCustom, calls=%fused_computation.1 | custom fusion | bytes 1052672 | tf_op jit(solution)/shard_map/gather | solution.py:102
  54.4 4.0 %gather_fusion.2 = f32[1024,128]{1,0:T(8,128)} fusion(f32[1025,128]{1,0:T(8,128)S(1)} %concatenate.55, s32[1024]{0:T(1024)S(1)} %broadcast_clamp_fusion), kind=kCustom, calls=%fused_computation.2 | custom fusion | bytes 1052672 | tf_op jit(solution)/shard_map/gather | solution.py:106
  58.4 9.7 %all-to-all-start.1 = ((f32[128,8,128]{2,1,0:T(8,128)}), f32[128,8,128]{2,1,0:T(8,128)S(1)}, u32[]{:S(2)}, u32[]{:S(2)}) async-start(f32[128,8,128]{2,1,0:T(8,128)} %bitcast.22), calls=%async_computation.1 | async-start | bytes 1048576 | tf_op jit(solution)/shard_map/all_to_all | solution.py:57
  68.2 8.3 %select_maximum_fusion.4 = f32[130,66,130]{2,1,0:T(8,128)} fusion(f32[130,1,128]{2,1,0:T(1,128)S(1)} %collective-permute-done.2, f32[130,64,128]{2,1,0:T(8,128)} %copy-done.2, f32[130,1,128]{2,1,0:T(1,128)S(1)} %collective-permute-done.3), kind=kLoop, calls=%fused_computation.14 | loop fusion | flops 8923200 | bytes 8854560 | tf_op jit(solution)/shard_map/concatenate | solution.py:18
  76.5 5.3 %all-to-all-done.1 = f32[128,8,128]{2,1,0:T(8,128)S(1)} async-done(((f32[128,8,128]{2,1,0:T(8,128)}), f32[128,8,128]{2,1,0:T(8,128)S(1)}, u32[]{:S(2)}, u32[]{:S(2)}) %all-to-all-start.1) | async-done | bytes 524320 | tf_op jit(solution)/shard_map/all_to_all | solution.py:57
  81.8 8.9 %scatter_custom_fusion = f32[8192,128]{1,0:T(8,128)} fusion(s32[1024]{0:T(1024)S(1)} %bitcast.108, f32[]{:T(128)} %constant.8.clone.1, f32[128,8,128]{2,1,0:T(8,128)S(1)} %all-to-all-done.1, s32[1024]{0:T(1024)S(1)} %lt.57, s32[1024]{0:T(1024)S(1)} %ge.30), kind=kCustom, calls=%fused_computation.87 | custom fusion | flops 655360 | bytes 4727808 | tf_op jit(solution)/shard_map/scatter-add | solution.py:116
  90.8 26.2 %fusion.35 = f32[128,64,128]{2,1,0:T(8,128)} fusion(f32[128,64,128]{2,1,0:T(8,128)} %bitcast.94, f32[128,64,128]{2,1,0:T(8,128)} %param.9, f32[1,64,128]{2,1,0:T(8,128)S(1)} %collective-permute-done.1, f32[1,64,128]{2,1,0:T(8,128)S(1)} %collective-permute-done, f32[130,1,128]{2,1,0:T(1,128)S(1)} %collective-permute-done.2, f32[130,64,128]{2,1,0:T(8,128)} %copy-done.2, ...), kind=kLoop, calls=%fused_computation.63 | loop fusion | flops 44040192 | bytes 46401536 | tf_op jit(solution)/shard_map/sub | solution.py:119
  116.9 5.0 %gather_fusion.3 = f32[1024,128]{1,0:T(8,128)S(1)} fusion(f32[8192,128]{1,0:T(8,128)} %bitcast.92, s32[1024]{0:T(1024)S(1)} %broadcast_clamp_fusion.2), kind=kCustom, calls=%fused_computation.3 | custom fusion | bytes 1052672 | tf_op jit(solution)/shard_map/gather | solution.py:95
  123.1 4.6 %all-to-all-start.2 = ((f32[128,8,128]{2,1,0:T(8,128)}), f32[128,8,128]{2,1,0:T(8,128)S(1)}, u32[]{:S(2)}, u32[]{:S(2)}) async-start(f32[128,8,128]{2,1,0:T(8,128)} %bitcast_select_fusion.2), calls=%async_computation.2 | async-start | bytes 1048576 | tf_op jit(solution)/shard_map/all_to_all | solution.py:53
  128.5 3.3 %collective-permute-start.5 = (f32[1,64,128]{2,1,0:T(8,128)S(1)}, f32[1,64,128]{2,1,0:T(8,128)S(1)}, u32[]{:S(2)}, u32[]{:S(2)}) collective-permute-start(f32[1,64,128]{2,1,0:T(8,128)S(1)} %get-tuple-element.8), channel_id=1, source_target_pairs={{0,8},{8,16},{16,24},{24,32},{32,40},{40,48},{48,56},{56,64},{64,7... | collective-permute-start | bytes 98312 | tf_op jit(solution)/shard_map/ppermute | solution.py:16
  138.3 4.5 %collective-permute-start.7 = (f32[130,1,128]{2,0,1:T(8,128)S(1)}, f32[130,1,128]{2,0,1:T(8,128)S(1)}, u32[]{:S(2)}, u32[]{:S(2)}) collective-permute-start(f32[130,1,128]{2,0,1:T(8,128)S(1)} %copy.48), channel_id=1, source_target_pairs={{0,1},{1,2},{2,3},{3,4},{4,5},{5,6},{6,7},{8,9},{9,10},{10,11},{11... | collective-permute-start | bytes 199688 | tf_op jit(solution)/shard_map/ppermute | solution.py:16
  144.9 3.6 %collective-permute-done.6 = f32[130,1,128]{2,0,1:T(8,128)S(1)} collective-permute-done((f32[130,1,128]{2,0,1:T(8,128)S(1)}, f32[130,1,128]{2,0,1:T(8,128)S(1)}, u32[]{:S(2)}, u32[]{:S(2)}) %collective-permute-start.6) | collective-permute-done | bytes 66592 | tf_op jit(solution)/shard_map/ppermute | solution.py:17
  152.1 4.0 %gather_fusion.5 = f32[1024,128]{1,0:T(8,128)} fusion(f32[1025,128]{1,0:T(8,128)S(1)} %concatenate.63, s32[1024]{0:T(1024)S(1)} %broadcast_clamp_fusion), kind=kCustom, calls=%fused_computation.5 | custom fusion | bytes 1052672 | tf_op jit(solution)/shard_map/gather | solution.py:106
  156.2 10.4 %all-to-all-start.3 = ((f32[128,8,128]{2,1,0:T(8,128)}), f32[128,8,128]{2,1,0:T(8,128)S(1)}, u32[]{:S(2)}, u32[]{:S(2)}) async-start(f32[128,8,128]{2,1,0:T(8,128)} %bitcast.31), calls=%async_computation.3 | async-start | bytes 1048576 | tf_op jit(solution)/shard_map/all_to_all | solution.py:57
  166.6 10.6 %select_maximum_fusion = f32[130,66,130]{2,1,0:T(8,128)} fusion(f32[130,1,128]{2,1,0:T(1,128)S(1)} %copy.47, f32[130,1,128]{2,1,0:T(1,128)S(1)} %copy.49, f32[1,64,128]{2,1,0:T(8,128)S(1)} %collective-permute-done.4, f32[128,64,128]{2,1,0:T(8,128)} %fusion.35, f32[1,64,128]{2,1,0:T(8,128)S(1)} %collective-permute-done.5), kind=kLoop, calls=%fused_computation.10 | loop fusion | flops 13384800 | bytes 8854560 | tf_op jit(solution)/shard_map/concatenate | solution.py:18
  177.2 3.1 %all-to-all-done.3 = f32[128,8,128]{2,1,0:T(8,128)S(1)} async-done(((f32[128,8,128]{2,1,0:T(8,128)}), f32[128,8,128]{2,1,0:T(8,128)S(1)}, u32[]{:S(2)}, u32[]{:S(2)}) %all-to-all-start.3) | async-done | bytes 524320 | tf_op jit(solution)/shard_map/all_to_all | solution.py:57
  180.3 8.9 %scatter_custom_fusion.1 = f32[8192,128]{1,0:T(8,128)} fusion(s32[1024]{0:T(1024)S(1)} %bitcast.109, f32[]{:T(128)} %constant.8.clone.1, f32[128,8,128]{2,1,0:T(8,128)S(1)} %all-to-all-done.3, s32[1024]{0:T(1024)S(1)} %lt.57, s32[1024]{0:T(1024)S(1)} %ge.30), kind=kCustom, calls=%fused_computation.85 | custom fusion | flops 655360 | bytes 4727808 | tf_op jit(solution)/shard_map/scatter-add | solution.py:116
  189.2 27.0 %fusion.11 = f32[128,64,128]{2,1,0:T(8,128)} fusion(f32[128,64,128]{2,1,0:T(8,128)} %bitcast.95, f32[128,64,128]{2,1,0:T(8,128)} %fusion.35, f32[1,64,128]{2,1,0:T(8,128)S(1)} %collective-permute-done.4, f32[1,64,128]{2,1,0:T(8,128)S(1)} %collective-permute-done.5, f32[130,1,128]{2,1,0:T(1,128)S(1)} %copy.49, f32[130,1,128]{2,1,0:T(1,128)S(1)} %copy.47, ...), kind=kLoop, calls=%fused_computation.30 | loop fusion | flops 48234496 | bytes 42141696 | tf_op jit(solution)/shard_map/sub | solution.py:119
  (68 shorter events, 25.2 us)
Async XLA Ops:
  0.6 53.1 %copy-start = (f32[1,1,32,32,32]{4,3,2,1,0:T(8,128)S(1)}, f32[1,1,32,32,32]{4,3,2,1,0:T(8,128)}, u32[]{:S(2)}) copy-start(f32[1,1,32,32,32]{4,3,2,1,0:T(8,128)} %param.17) | copy-start | bytes 393220
  0.6 29.0 %copy-start.5 = (s32[1,1,128,8]{2,3,1,0:T(8,128)S(1)}, s32[1,1,128,8]{2,3,1,0:T(8,128)}, u32[]{:S(2)}) copy-start(s32[1,1,128,8]{2,3,1,0:T(8,128)} %param.14) | copy-start | bytes 12292
  0.7 28.8 %copy-start.4 = (s32[1,1,128,8]{2,3,1,0:T(8,128)S(1)}, s32[1,1,128,8]{2,3,1,0:T(8,128)}, u32[]{:S(2)}) copy-start(s32[1,1,128,8]{2,3,1,0:T(8,128)} %param.13) | copy-start | bytes 12292
  0.7 28.8 %copy-start.6 = (s32[1,1,1024]{2,1,0:T(1,128)S(1)}, s32[1,1,1024]{2,1,0:T(1,128)}, u32[]{:S(2)}) copy-start(s32[1,1,1024]{2,1,0:T(1,128)} %param.15) | copy-start | bytes 12292
  0.7 28.8 %copy-start.7 = (s32[1,1,1024]{2,1,0:T(1,128)S(1)}, s32[1,1,1024]{2,1,0:T(1,128)}, u32[]{:S(2)}) copy-start(s32[1,1,1024]{2,1,0:T(1,128)} %param.16) | copy-start | bytes 12292
  1.5 41.6 %collective-permute-start = (f32[1,64,128]{2,1,0:T(8,128)S(1)}, f32[1,64,128]{2,1,0:T(8,128)S(1)}, u32[]{:S(2)}, u32[]{:S(2)}) collective-permute-start(f32[1,64,128]{2,1,0:T(8,128)S(1)} %get-tuple-element.10), channel_id=1, source_target_pairs={{8,0},{16,8},{24,16},{32,24},{40,32},{48,40},{56,48},{64,56},{72,6... | collective-permute-start | bytes 98312 | tf_op jit(solution)/shard_map/ppermute | solution.py:17
  2.8 40.0 %collective-permute-start.1 = (f32[1,64,128]{2,1,0:T(8,128)S(1)}, f32[1,64,128]{2,1,0:T(8,128)S(1)}, u32[]{:S(2)}, u32[]{:S(2)}) collective-permute-start(f32[1,64,128]{2,1,0:T(8,128)S(1)} %get-tuple-element.11), channel_id=1, source_target_pairs={{0,8},{8,16},{16,24},{24,32},{32,40},{40,48},{48,56},{56,64},{64,7... | collective-permute-start | bytes 98312 | tf_op jit(solution)/shard_map/ppermute | solution.py:16
  16.1 34.7 %all-to-all-start = ((f32[128,8,128]{2,1,0:T(8,128)}), f32[128,8,128]{2,1,0:T(8,128)S(1)}, u32[]{:S(2)}, u32[]{:S(2)}) async-start(f32[128,8,128]{2,1,0:T(8,128)} %bitcast_select_fusion.5), calls=%async_computation | async-start | bytes 1048576 | tf_op jit(solution)/shard_map/all_to_all | solution.py:53
  29.8 6.9 %slice-start = ((s8[6291456]{0:T(1024)(128)(4,1)}), s8[2097152]{0:T(1024)(128)(4,1)S(1)}, s32[]{:S(2)}) async-start(s8[6291456]{0:T(1024)(128)(4,1)} %bitcast.96), calls=%async_computation.4 | async-start | bytes 4194304
  29.9 6.8 %slice-start.1 = ((s8[6291456]{0:T(1024)(128)(4,1)}), s8[4194304]{0:T(1024)(128)(4,1)S(1)}, s32[]{:S(2)}) async-start(s8[6291456]{0:T(1024)(128)(4,1)} %bitcast.96), calls=%async_computation.5 | async-start | bytes 8388608
  36.7 6.1 %copy-start.1 = (f32[128,64,128]{2,1,0:T(8,128)S(1)}, f32[128,64,128]{2,1,0:T(8,128)}, u32[]{:S(2)}) copy-start(f32[128,64,128]{2,1,0:T(8,128)} %param.9) | copy-start | bytes 12582916
  43.2 2.0 copy-start.2
  45.2 22.9 %collective-permute-start.3 = (f32[130,1,128]{2,1,0:T(1,128)S(1)}, f32[130,1,128]{2,1,0:T(1,128)S(1)}, u32[]{:S(2)}, u32[]{:S(2)}) collective-permute-start(f32[130,1,128]{2,1,0:T(1,128)S(1)} %get-tuple-element.6), channel_id=1, source_target_pairs={{0,1},{1,2},{2,3},{3,4},{4,5},{5,6},{6,7},{8,9},{9,10},{10,11},{11... | collective-permute-start | bytes 199688 | tf_op jit(solution)/shard_map/ppermute | solution.py:16
  48.9 19.3 %collective-permute-start.2 = (f32[130,1,128]{2,1,0:T(1,128)S(1)}, f32[130,1,128]{2,1,0:T(1,128)S(1)}, u32[]{:S(2)}, u32[]{:S(2)}) collective-permute-start(f32[130,1,128]{2,1,0:T(1,128)S(1)} %get-tuple-element.7), channel_id=1, source_target_pairs={{1,0},{2,1},{3,2},{4,3},{5,4},{6,5},{7,6},{9,8},{10,9},{11,10},{12... | collective-permute-start | bytes 199688 | tf_op jit(solution)/shard_map/ppermute | solution.py:17
  58.4 23.4 %all-to-all-start.1 = ((f32[128,8,128]{2,1,0:T(8,128)}), f32[128,8,128]{2,1,0:T(8,128)S(1)}, u32[]{:S(2)}, u32[]{:S(2)}) async-start(f32[128,8,128]{2,1,0:T(8,128)} %bitcast.22), calls=%async_computation.1 | async-start | bytes 1048576 | tf_op jit(solution)/shard_map/all_to_all | solution.py:57
  123.1 25.5 %all-to-all-start.2 = ((f32[128,8,128]{2,1,0:T(8,128)}), f32[128,8,128]{2,1,0:T(8,128)S(1)}, u32[]{:S(2)}, u32[]{:S(2)}) async-start(f32[128,8,128]{2,1,0:T(8,128)} %bitcast_select_fusion.2), calls=%async_computation.2 | async-start | bytes 1048576 | tf_op jit(solution)/shard_map/all_to_all | solution.py:53
  128.5 6.2 %collective-permute-start.5 = (f32[1,64,128]{2,1,0:T(8,128)S(1)}, f32[1,64,128]{2,1,0:T(8,128)S(1)}, u32[]{:S(2)}, u32[]{:S(2)}) collective-permute-start(f32[1,64,128]{2,1,0:T(8,128)S(1)} %get-tuple-element.8), channel_id=1, source_target_pairs={{0,8},{8,16},{16,24},{24,32},{32,40},{40,48},{48,56},{56,64},{64,7... | collective-permute-start | bytes 98312 | tf_op jit(solution)/shard_map/ppermute | solution.py:16
  131.8 5.2 %collective-permute-start.4 = (f32[1,64,128]{2,1,0:T(8,128)S(1)}, f32[1,64,128]{2,1,0:T(8,128)S(1)}, u32[]{:S(2)}, u32[]{:S(2)}) collective-permute-start(f32[1,64,128]{2,1,0:T(8,128)S(1)} %get-tuple-element.9), channel_id=1, source_target_pairs={{8,0},{16,8},{24,16},{32,24},{40,32},{48,40},{56,48},{64,56},{72,6... | collective-permute-start | bytes 98312 | tf_op jit(solution)/shard_map/ppermute | solution.py:17
  138.3 6.5 %collective-permute-start.7 = (f32[130,1,128]{2,0,1:T(8,128)S(1)}, f32[130,1,128]{2,0,1:T(8,128)S(1)}, u32[]{:S(2)}, u32[]{:S(2)}) collective-permute-start(f32[130,1,128]{2,0,1:T(8,128)S(1)} %copy.48), channel_id=1, source_target_pairs={{0,1},{1,2},{2,3},{3,4},{4,5},{5,6},{6,7},{8,9},{9,10},{10,11},{11... | collective-permute-start | bytes 199688 | tf_op jit(solution)/shard_map/ppermute | solution.py:16
  142.9 5.6 %collective-permute-start.6 = (f32[130,1,128]{2,0,1:T(8,128)S(1)}, f32[130,1,128]{2,0,1:T(8,128)S(1)}, u32[]{:S(2)}, u32[]{:S(2)}) collective-permute-start(f32[130,1,128]{2,0,1:T(8,128)S(1)} %copy.46), channel_id=1, source_target_pairs={{1,0},{2,1},{3,2},{4,3},{5,4},{6,5},{7,6},{9,8},{10,9},{11,10},{12... | collective-permute-start | bytes 199688 | tf_op jit(solution)/shard_map/ppermute | solution.py:17
  152.1 25.1 %copy-start.3 = (f32[32,128,32]{1,2,0:T(8,128)}, f32[32,128,32]{1,2,0:T(8,128)S(1)}, u32[]{:S(2)}) copy-start(f32[32,128,32]{1,2,0:T(8,128)S(1)} %fusion.47) | copy-start | bytes 1572868
  156.2 24.1 %all-to-all-start.3 = ((f32[128,8,128]{2,1,0:T(8,128)}), f32[128,8,128]{2,1,0:T(8,128)S(1)}, u32[]{:S(2)}, u32[]{:S(2)}) async-start(f32[128,8,128]{2,1,0:T(8,128)} %bitcast.31), calls=%async_computation.3 | async-start | bytes 1048576 | tf_op jit(solution)/shard_map/all_to_all | solution.py:57
where the time goes:
time: 217 us; the launch traced here: 216 us
  other arithmetic  106 us (49%)
  starting transfers between devices  60.6 us (28%)
  local copies, waits for them, and re-layouts  30.9 us (14%)
  waiting for transfers between devices  16 us (7%)
    sub x2, other arithmetic, local(): thermal_state + rate  53.2 us
    all_to_all x2, starting transfers between devices, send_rates(): lax.all_to_all(block, ('gx', 'gy'), split_axis=0, concat_axis=0, tiled=True)  20.2 us
    concatenate x2, other arithmetic, extended_2(): x = jnp.concatenate([before, x, after], axis=dim)  18.9 us
    all_to_all x2, starting transfers between devices, send_columns(): lax.all_to_all(block, ('gx', 'gy'), split_axis=0, concat_axis=0, tiled=True)  17.9 us
    scatter-add x2, other arithmetic, local(): deposit = jnp.zeros((patch_extent_east * patch_extent_north, stratum_thic...  17.8 us
    ppermute x4, starting transfers between devices, extended_2(): before = lax.ppermute(last, axis, up)  16.1 us
    gather x2, local copies, waits for them, and re-layouts, local(): columns = flat_field[cells] * masks  9.99 us
    all_to_all x2, waiting for transfers between devices, send_rates(): lax.all_to_all(block, ('gx', 'gy'), split_axis=0, concat_axis=0, tiled=True)  8.4 us
  transfers between devices with their start and end apart: 12, of which 5 were waited for; matrix products, arithmetic and copies ran while one was open for 24% of the time, Pallas kernels for 0%

commit v1 on v0

v1 whole, which is shorter than its diff:
```python
import functools

import jax
import jax.numpy as jnp
from jax import lax
from jax.experimental import pallas as pl
from jax.experimental.pallas import tpu as pltpu
from jax.sharding import PartitionSpec as P

MESH = pl.DeviceIdType.MESH
F32 = jnp.float32
BF16 = jnp.bfloat16

NX, NY, NZ = 128, 64, 128
CELLS = NX * NY
GROUPS, CAP = 128, 8
SLOTS = GROUPS * CAP
HALF = 64

HOPS = (0, 1, 2, 1)
OFFSETS = sorted(
    [(a, b, c, d) for a in range(4) for b in range(4) for c in range(4) for d in range(2)][1:],
    key=lambda o: -(HOPS[o[0]] + HOPS[o[1]] + HOPS[o[2]] + 0.3 * o[3]),
)


def iota(shape, dim):
    return lax.broadcasted_iota(jnp.int32, shape, dim)


def dot(a, b):
    return jnp.dot(a, b, preferred_element_type=F32)


def parts_of(x):
    hi = x.astype(BF16)
    return hi, (x - hi.astype(F32)).astype(BF16)


def one_hot(mask):
    return jnp.where(mask, 1.0, 0.0).astype(BF16)


def spread(table, first_lane):
    slot, lane = iota((SLOTS, 128), 0), iota((SLOTS, 128), 1)
    rows = dot(one_hot(slot // CAP == lane), table.astype(BF16))
    own = jnp.where(lane == first_lane + slot % CAP, rows, 0.0).astype(BF16)
    return dot(own, jnp.ones((128, 128), BF16)).astype(jnp.int32)


def rate_of(c, xm, xp, ym, yp, flux, mix):
    vx, vy, vz = flux
    kh, kv = mix
    lane = iota((NY, NZ), 1)
    zm = jnp.where(lane == 0, 0.0, pltpu.roll(c, 1, 1))
    zp = jnp.where(lane == NZ - 1, 0.0, pltpu.roll(c, NZ - 1, 1))
    total = (kh - jnp.minimum(vx, 0.0)) * (xp - c) - (kh + jnp.maximum(vx, 0.0)) * (c - xm)
    total += (kh - jnp.minimum(vy, 0.0)) * (yp - c) - (kh + jnp.maximum(vy, 0.0)) * (c - ym)
    total += (kv - jnp.minimum(vz, 0.0)) * (zp - c) - (kv + jnp.maximum(vz, 0.0)) * (c - zm)
    return c + 0.1 * total


def transport(
    site,
    u_hbm,
    flux_hbm,
    mix_hbm,
    first_ref,
    stop_ref,
    site_row,
    lookup_row,
    order_row,
    solver_ref,
    grid_out,
    columns_out,
    heat_out,
    state,
    after,
    flux,
    mix,
    xhalo,
    yhalo,
    yface,
    columns,
    base,
    masks,
    pack_own,
    unpack_own,
    pack_got,
    unpack_got,
    table,
    lookup_mat,
    return_mat,
    cell_mat,
    blocks,
    rhs,
    out_box,
    in_box,
    out_one,
    in_one,
    load_sem,
    store_sem,
    halo_send,
    halo_recv,
    send_sem,
    recv_sem,
):
    gx, gy = lax.axis_index("gx"), lax.axis_index("gy")
    me = gx * 8 + gy
    px, py = lax.div(gx, 4), lax.rem(gx, 4)
    pz, pc = lax.div(gy, 2), lax.rem(gy, 2)
    xs = [lax.rem(px + i, 4) for i in range(4)]
    ys = [lax.rem(py + i, 4) for i in range(4)]
    zs = [lax.rem(pz + i, 4) for i in range(4)]
    cs = [lax.rem(pc + i, 2) for i in range(2)]
    peers = [(xs[a] * 4 + ys[b], zs[c] * 2 + cs[d]) for a, b, c, d in OFFSETS]

    load_u = pltpu.make_async_copy(u_hbm, state, load_sem.at[0])
    load_flux = pltpu.make_async_copy(flux_hbm, flux, load_sem.at[1])
    load_mix = pltpu.make_async_copy(mix_hbm, mix, load_sem.at[2])
    load_u.start()
    load_flux.start()
    load_mix.start()
    barrier = pltpu.get_barrier_semaphore()
    for peer in peers:
        pl.semaphore_signal(barrier, inc=1, device_id=peer, device_id_type=MESH)

    lane8 = iota((CAP, 128), 1)

    def pack(index, box, width):
        def group(o, carry):
            rows = pl.ds(pl.multiple_of(o * CAP, CAP), CAP)
            cut = jnp.take_along_axis(columns[rows, :], index[rows, :], axis=1)
            box[o, 0:4, :] = jnp.where(lane8[0:4] < HALF, cut[0:4], cut[4:8])
            return carry

        lax.fori_loop(0, GROUPS, group, 0, unroll=8)

    def unpack(box, index, keep):
        def group(o, carry):
            rows = pl.ds(pl.multiple_of(o * CAP, CAP), CAP)
            half = box[o, 0:4, :]
            both = jnp.concatenate([half, half], axis=0)
            wide = jnp.take_along_axis(both, index[rows, :], axis=1)
            wide = wide * keep(rows)
            columns[rows, :] = wide
            return carry

        lax.fori_loop(0, GROUPS, group, 0, unroll=8)

    def indices(first, pack_ref, unpack_ref):
        lane = iota((SLOTS, 128), 1)
        shift = jnp.where(iota((SLOTS, 128), 0) % CAP >= 4, HALF, 0)
        pack_ref[...] = (lane + first + shift) & 127
        unpack_ref[...] = (lane - first + shift) & 127

    def send(box, landing, k):
        for x, y in peers:
            pltpu.make_async_remote_copy(
                box.at[x * 8 + y],
                landing.at[me],
                send_sem.at[k],
                recv_sem.at[k],
                device_id=(x, y),
                device_id_type=MESH,
            ).start()
        landing[me] = box[me]

    def receive(box, landing, k):
        some = landing.at[pl.ds(0, GROUPS - 1)]
        pltpu.make_async_copy(some, some, recv_sem.at[k]).wait()

    def sent(box, k):
        some = box.at[pl.ds(0, GROUPS - 1)]
        pltpu.make_async_copy(some, some, send_sem.at[k]).wait()

    def halo_copies(step):
        low_x, high_x = state.at[pl.ds(0, NY)], state.at[pl.ds(CELLS - NY, NY)]
        low_y, high_y = yface.at[step, 0], yface.at[step, 1]
        plan = [
            (gx > 0, low_x, xhalo.at[step, 1], 1, (gx - 1, gy)),
            (gx < 15, high_x, xhalo.at[step, 0], 0, (gx + 1, gy)),
            (gy > 0, low_y, yhalo.at[step, 1], 3, (gx, gy - 1)),
            (gy < 7, high_y, yhalo.at[step, 0], 2, (gx, gy + 1)),
        ]
        return [
            (
                there,
                pltpu.make_async_remote_copy(
                    source,
                    target,
                    halo_send.at[step, side],
                    halo_recv.at[step, side],
                    device_id=device,
                    device_id_type=MESH,
                ),
            )
            for there, source, target, side, device in plan
        ]

    def halo_start(step):
        def face(i, carry):
            yface[step, 0, pl.ds(i, 1), :] = state[pl.ds(i * NY, 1), :]
            yface[step, 1, pl.ds(i, 1), :] = state[pl.ds(i * NY + NY - 1, 1), :]
            return carry

        lax.fori_loop(0, NX, face, 0, unroll=8)
        for there, copy in halo_copies(step):

            @pl.when(there)
            def _():
                copy.start()

    def halo_wait(step):
        for there, copy in halo_copies(step):

            @pl.when(there)
            def _():
                copy.wait_send()

        for there, side in ((gx > 0, 0), (gx < 15, 1), (gy > 0, 2), (gy < 7, 3)):
            block = xhalo.at[step, side] if side < 2 else yhalo.at[step, side - 2]

            @pl.when(there)
            def _():
                pltpu.make_async_copy(block, block, halo_recv.at[step, side]).wait()

    def stencil(step):
        row = iota((NY, NZ), 0)

        def slab(i, xm, xp):
            here = pl.ds(pl.multiple_of(i * NY, NY), NY)
            c = state[here, :]
            ym = jnp.where(row == 0, yhalo[step, 0, pl.ds(i, 1), :], pltpu.roll(c, 1, 0))
            yp = jnp.where(row == NY - 1, yhalo[step, 1, pl.ds(i, 1), :], pltpu.roll(c, NY - 1, 0))
            after[here, :] = rate_of(
                c,
                xm,
                xp,
                ym,
                yp,
                [flux[d, here, :].astype(F32) for d in range(3)],
                [mix[d, here, :].astype(F32) for d in range(2)],
            )

        def at(i):
            return state[pl.ds(pl.multiple_of(i * NY, NY), NY), :]

        def inner(i, carry):
            slab(i, at(i - 1), at(i + 1))
            return carry

        slab(0, xhalo[step, 0], at(1))
        lax.fori_loop(1, NX - 1, inner, 0)
        slab(NX - 1, at(NX - 2), xhalo[step, 1])

    def gather(source, target):
        def group(o, carry):
            for c in range(CAP):
                s = o * CAP + c
                target[pl.ds(s, 1), :] = source[pl.ds(site[s], 1), :]
            return carry

        lax.fori_loop(0, GROUPS, group, 0, unroll=4)

    def solve(last):
        hi, lo = parts_of(columns[...])
        rhs[:, 0:128] = hi
        rhs[:, 128:256] = lo
        loops = dot(lookup_mat[...], rhs[...]).astype(BF16)
        for g in range(4):
            rows = slice(g * 256, g * 256 + 256)
            two = dot(blocks[0, rows, :], loops[rows])
            small = dot(blocks[1, rows, :], loops[rows, 0:128])
            rates = two[:, 0:128] + two[:, 128:256] + small
            if last:
                heat_out[rows, :] = rates
            hi, lo = parts_of(rates)
            rhs[rows, 0:128] = hi
            rhs[rows, 128:256] = lo
        two = dot(return_mat[...], rhs[...])
        columns[...] = two[:, 0:128] + two[:, 128:256]

    def deposits():
        hi, lo = parts_of(columns[...])
        rhs[:, 0:128] = hi
        rhs[:, 128:256] = lo
        two = dot(cell_mat[...], rhs[...])
        return two[:, 0:128] + two[:, 128:256]

    table[...] = jnp.zeros_like(table)
    table[:, 0:8] = first_ref[...].astype(F32)
    table[:, 8:16] = stop_ref[...].astype(F32)
    first = spread(table[...], 0)
    stop = spread(table[...], 8)
    layer = iota((SLOTS, 128), 1)
    masks[...] = jnp.where((layer >= first) & (layer < stop), 1.0, 0.0)
    indices(first, pack_own, unpack_own)
    for edge, halo, side in ((gx == 0, xhalo, 0), (gx == 15, xhalo, 1), (gy == 0, yhalo, 0), (gy == 7, yhalo, 1)):

        @pl.when(edge)
        def _():
            halo[:, side] = jnp.zeros_like(halo[:, side])

    load_u.wait()
    gather(state, columns)
    columns[...] = columns[...] * masks[...]
    pack(pack_own, out_one, 5)
    out_one[:, 4, :] = table[...]
    pl.semaphore_wait(barrier, GROUPS - 1)
    halo_start(0)
    send(out_one, in_one, 0)

    def build(o, carry):
        rows = pl.ds(pl.multiple_of(o * 128, 128), 128)
        slot = iota((128, SLOTS), 0) + o * 128
        lookup_mat[rows, :] = one_hot(order_row[...] == slot)
        return_mat[rows, :] = one_hot(lookup_row[...] == slot)
        return carry

    lax.fori_loop(0, 8, build, 0)
    tile = one_hot(iota((32, 256), 1) % 32 == iota((32, 256), 0))
    own_block = (iota((SLOTS, 256), 0) // 32) % 8 == iota((SLOTS, 256), 1) // 32
    for part, piece in enumerate(parts_of(solver_ref[...])):
        blocks[part] = jnp.where(own_block, dot(piece, tile), 0.0).astype(BF16)
    ones = jnp.ones((128, 128), BF16)

    load_flux.wait()
    load_mix.wait()
    halo_wait(0)
    stencil(0)
    receive(out_one, in_one, 0)
    indices(spread(in_one[:, 4, :], 0), pack_got, unpack_got)
    window = lambda index: lambda rows: jnp.where(
        ((index[rows, :] ^ jnp.where(iota((CAP, 128), 0) >= 4, HALF, 0)) & 127) < HALF, 1.0, 0.0
    )
    keep_got = window(unpack_got)
    keep_own = lambda rows: masks[rows, :]
    unpack(in_one, unpack_got, keep_got)
    solve(False)
    pack(pack_got, out_box.at[0], 4)
    send(out_box.at[0], in_box.at[0], 1)

    gather(after, base)

    eye = iota((128, 128), 0) == iota((128, 128), 1)
    for o in range(8):
        piece = site_row[:, o * 128 : (o + 1) * 128]
        upper = jnp.where(eye, lax.shift_right_logical(piece, 6).astype(F32), 0.0).astype(BF16)
        lower = jnp.where(eye, (piece & 63).astype(F32), 0.0).astype(BF16)
        tall = (dot(upper, ones) * 64.0 + dot(lower, ones)).astype(jnp.int32)
        for q in range(8):
            cell_mat[o * 128 : (o + 1) * 128, q * 128 : (q + 1) * 128] = one_hot(
                tall == site_row[:, q * 128 : (q + 1) * 128]
            )

    receive(out_box.at[0], in_box.at[0], 1)
    unpack(in_box.at[0], unpack_own, keep_own)
    base[...] = base[...] - deposits()
    columns[...] = base[...] * masks[...]
    pack(pack_own, out_box.at[1], 4)
    send(out_box.at[1], in_box.at[1], 2)

    def lay(o, carry):
        rows = pl.ds(pl.multiple_of(o * 1024, 1024), 1024)
        pick = one_hot(iota((1024, SLOTS), 0) + o * 1024 == site_row[...])
        two = dot(pick, rhs[...])
        state[rows, :] = after[rows, :] - (two[:, 0:128] + two[:, 128:256])
        return carry

    lax.fori_loop(0, 8, lay, 0)
    halo_start(1)
    receive(out_box.at[1], in_box.at[1], 2)
    unpack(in_box.at[1], unpack_got, keep_got)
    solve(True)
    pack(pack_got, out_box.at[2], 4)
    send(out_box.at[2], in_box.at[2], 3)

    halo_wait(1)
    stencil(1)
    store = pltpu.make_async_copy(after, grid_out, store_sem)
    store.start()
    gather(after, base)
    receive(out_box.at[2], in_box.at[2], 3)
    unpack(in_box.at[2], unpack_own, keep_own)
    columns_out[...] = base[...] - deposits()
    sent(out_one, 0)
    for k in range(3):
        sent(out_box.at[k], k + 1)
    store.wait()


def settle(site, grid_hbm, rows_ref, heat_hbm, out_hbm, heat_out, held, sem):
    heat = pltpu.make_async_copy(heat_hbm, heat_out, sem.at[2])
    heat.start()
    load = pltpu.make_async_copy(grid_hbm, held, sem.at[0])
    load.start()
    load.wait()

    def group(o, carry):
        for c in range(CAP):
            s = o * CAP + c
            held[pl.ds(site[s], 1), :] = rows_ref[pl.ds(s, 1), :]
        return carry

    lax.fori_loop(0, GROUPS, group, 0, unroll=4)
    store = pltpu.make_async_copy(held, out_hbm, sem.at[1])
    store.start()
    store.wait()
    heat.wait()


VMEM = pl.BlockSpec(memory_space=pltpu.VMEM)
SMEM = pl.BlockSpec(memory_space=pltpu.SMEM)
ANY = pl.BlockSpec(memory_space=pl.ANY)


def local(u, flux, mix, site, first, stop, lookup, order, solver):
    u2 = u.reshape(CELLS, NZ)
    flux2 = flux.reshape(3, CELLS, NZ)
    mix2 = mix.reshape(2, CELLS, NZ)
    site1 = site.reshape(SLOTS)
    grid_shape = jax.ShapeDtypeStruct((CELLS, NZ), F32)
    slot_shape = jax.ShapeDtypeStruct((SLOTS, NZ), F32)
    slot_f32 = pltpu.VMEM((SLOTS, NZ), F32)
    slot_i32 = pltpu.VMEM((SLOTS, NZ), jnp.int32)
    square = pltpu.VMEM((SLOTS, SLOTS), BF16)
    grid, rows, heat = pl.pallas_call(
        transport,
        out_shape=(grid_shape, slot_shape, slot_shape),
        in_specs=[SMEM, ANY, ANY, ANY] + [VMEM] * 6,
        out_specs=(ANY, VMEM, VMEM),
        scratch_shapes=[
            pltpu.VMEM((CELLS, NZ), F32),
            pltpu.VMEM((CELLS, NZ), F32),
            pltpu.VMEM((3, CELLS, NZ), BF16),
            pltpu.VMEM((2, CELLS, NZ), BF16),
            pltpu.VMEM((2, 2, NY, NZ), F32),
            pltpu.VMEM((2, 2, NX, NZ), F32),
            pltpu.VMEM((2, 2, NX, NZ), F32),
            slot_f32,
            slot_f32,
            slot_f32,
            slot_i32,
            slot_i32,
            slot_i32,
            slot_i32,
            pltpu.VMEM((GROUPS, 128), F32),
            square,
            square,
            square,
            pltpu.VMEM((2, SLOTS, 256), BF16),
            pltpu.VMEM((SLOTS, 256), BF16),
            pltpu.VMEM((3, GROUPS, 4, NZ), F32),
            pltpu.VMEM((3, GROUPS, 4, NZ), F32),
            pltpu.VMEM((GROUPS, 5, NZ), F32),
            pltpu.VMEM((GROUPS, 5, NZ), F32),
            pltpu.SemaphoreType.DMA((3,)),
            pltpu.SemaphoreType.DMA,
            pltpu.SemaphoreType.DMA((2, 4)),
            pltpu.SemaphoreType.DMA((2, 4)),
            pltpu.SemaphoreType.DMA((4,)),
            pltpu.SemaphoreType.DMA((4,)),
        ],
        compiler_params=pltpu.CompilerParams(
            collective_id=0, has_side_effects=True, vmem_limit_bytes=56 << 20
        ),
    )(
        site1,
        u2,
        flux2,
        mix2,
        first.reshape(GROUPS, CAP),
        stop.reshape(GROUPS, CAP),
        site1.reshape(1, SLOTS),
        lookup.reshape(1, SLOTS),
        order.reshape(1, SLOTS),
        solver.reshape(SLOTS, 32),
    )
    grid, heat = pl.pallas_call(
        settle,
        out_shape=(grid_shape, slot_shape),
        in_specs=[SMEM, ANY, VMEM, ANY],
        out_specs=(ANY, ANY),
        scratch_shapes=[pltpu.VMEM((CELLS, NZ), F32), pltpu.SemaphoreType.DMA((3,))],
        compiler_params=pltpu.CompilerParams(vmem_limit_bytes=16 << 20),
    )(site1, grid, rows, heat)
    return grid.reshape(NX, NY, NZ), heat.reshape(1, 1, SLOTS, NZ)


def solution(mesh):
    placed = (
        P("gx", "gy", None),
        P(None, "gx", "gy", None),
        P(None, "gx", "gy", None),
        P("gx", "gy", None, None),
        P("gx", "gy", None, None),
        P("gx", "gy", None, None),
        P("gx", "gy", None),
        P("gx", "gy", None),
        P("gx", "gy", None, None, None),
    )
    return jax.shard_map(
        local,
        mesh=mesh,
        in_specs=placed,
        out_specs=(P("gx", "gy", None), P("gx", "gy", None, None)),
        check_vma=False,
    )
```

time: 217 us -> 89.8 us (0.41)
  other arithmetic: 106 us -> 0 us
  Pallas kernels: 0 us -> 79.6 us
  starting transfers between devices: 60.6 us -> 0 us
  local copies, waits for them, and re-layouts: 30.9 us -> 9.25 us
  waiting for transfers between devices: 16 us -> 0 us
    pallas_call x0 -> x2, Pallas kernels: none -> 79.6 us  [the longest x1 75.7 us: local(): pl.pallas_call(transport, out_shape=(grid_shape, slot_shape, slot_shape),...]
    sub x2 -> x0, other arithmetic: 53.2 us -> none  [local(): thermal_state + rate]
    all_to_all x4 -> x0, starting transfers between devices: 38.1 us -> none  [the longest x2 20.2 us: send_rates(): lax.all_to_all(block, ('gx', 'gy'), split_axis=0, concat_axis=0, tiled=True)]
    gather x6 -> x0, local copies, waits for them, and re-layouts: 23.7 us -> none  [the longest x2 9.99 us: local(): columns = flat_field[cells] * masks]
    ppermute x8 -> x0, starting transfers between devices: 22.6 us -> none  [the longest x4 16.1 us: extended_2(): before = lax.ppermute(last, axis, up)]
    concatenate x2 -> x0, other arithmetic: 18.9 us -> none  [extended_2(): x = jnp.concatenate([before, x, after], axis=dim)]
    scatter-add x2 -> x0, other arithmetic: 17.8 us -> none  [local(): deposit = jnp.zeros((patch_extent_east * patch_extent_north, stratum_thic...]
    convert_element_type x2 -> x0, other arithmetic: 12.9 us -> none  [the longest x1 6.76 us: tendency(): coeff = mixing_coefficient.astype(jnp.float32)]
  transfers between devices with their start and end apart: 12 -> 0, of which waited for: 5 -> 0; matrix products, arithmetic and copies ran while one was open for 24% -> 0% of each run, Pallas kernels for 0% -> 0%
where the time goes in v1:
time: 89.8 us; the launch traced here: 89.5 us
  Pallas kernels  79.6 us (89%)
  local copies, waits for them, and re-layouts  9.25 us (10%)
    pallas_call x1, Pallas kernels, local(): pl.pallas_call(transport, out_shape=(grid_shape, slot_shape, slot_shape),...  75.7 us
    unnamed x11, local copies, waits for them, and re-layouts  7.88 us
    pallas_call x1, Pallas kernels, local(): pl.pallas_call(settle, out_shape=(grid_shape, slot_shape), in_specs=[SMEM...  3.91 us

profile of v1, /device:TPU:1, one launch (start us, length us, event | category | flops | bytes accessed | tf_op | source)
XLA Modules:
  0.0 89.5 jit_solution(13527394146681817927)
XLA Ops:
  0.6 0.8 copy.14
  1.4 0.7 reshape.37.site
  2.1 0.7 reshape_reshape.3.site_row
  2.8 1.4 %copy.15 = s32[1,1,128,8]{3,2,1,0:T(8,128)} copy(s32[1,1,128,8]{2,3,1,0:T(8,128)} %param.13) | data formatting | bytes 8192 | tf_op args[4]
  4.2 1.4 %copy.16 = s32[1,1,128,8]{3,2,1,0:T(8,128)} copy(s32[1,1,128,8]{2,3,1,0:T(8,128)} %param.14) | data formatting | bytes 8192 | tf_op args[5]
  5.6 0.0 copy-start.3
  5.6 75.7 %shard_map.104 = (f32[8192,128]{1,0:T(8,128)}, f32[1024,128]{1,0:T(8,128)}, f32[1024,128]{1,0:T(8,128)}) custom-call(s32[1024]{0:T(1024)} %reshape.37.site, f32[8192,128]{1,0:T(8,128)} %bitcast.15, bf16[3,8192,128]{2,1,0:T(8,128)(2,1)} %bitcast.14, bf16[2,8192,128]{2,1,0:T(8,128)(2,1)} %bitcast.16, s32[128,8]{1,0:T(8,128)} %bitcast.18, s32[128,8]{1,0:T(8,128)} %bitcast.19, ...), custom_call_target="tpu_custom_call" | custom-call | tf_op jit(solution)/shard_map/pallas_call | solution.py:428
  81.3 0.0 copy-done.3
  81.3 0.0 copy-start
  81.3 2.2 %copy-done = f32[8192,128]{1,0:T(8,128)S(1)} copy-done((f32[8192,128]{1,0:T(8,128)S(1)}, f32[8192,128]{1,0:T(8,128)}, u32[]{:S(2)}) %copy-start) | copy-done | bytes 4194328
  83.5 0.0 copy-start.1
  83.5 1.0 %copy-done.1 = f32[1024,128]{1,0:T(8,128)S(1)} copy-done((f32[1024,128]{1,0:T(8,128)S(1)}, f32[1024,128]{1,0:T(8,128)}, u32[]{:S(2)}) %copy-start.1) | copy-done | bytes 524312
  84.5 0.0 copy-start.2
  84.5 1.0 %copy-done.2 = f32[1024,128]{1,0:T(8,128)S(1)} copy-done((f32[1024,128]{1,0:T(8,128)S(1)}, f32[1024,128]{1,0:T(8,128)}, u32[]{:S(2)}) %copy-start.2) | copy-done | bytes 524312
  85.6 3.9 %shard_map.105 = (f32[8192,128]{1,0:T(8,128)}, f32[1024,128]{1,0:T(8,128)}) custom-call(s32[1024]{0:T(1024)S(1)} %copy-done.3, f32[8192,128]{1,0:T(8,128)S(1)} %copy-done, f32[1024,128]{1,0:T(8,128)S(1)} %copy-done.1, f32[1024,128]{1,0:T(8,128)S(1)} %copy-done.2), custom_call_target="tpu_custom_call" | custom-call | tf_op jit(solution)/shard_map/pallas_call | solution.py:480
Async XLA Ops:
  5.6 75.7 %copy-start.3 = (s32[1024]{0:T(1024)S(1)}, s32[1024]{0:T(1024)}, u32[]{:S(2)}) copy-start(s32[1024]{0:T(1024)} %reshape.37.site) | copy-start | bytes 12292
  81.3 2.2 %copy-start = (f32[8192,128]{1,0:T(8,128)S(1)}, f32[8192,128]{1,0:T(8,128)}, u32[]{:S(2)}) copy-start(f32[8192,128]{1,0:T(8,128)} %get-tuple-element.7.grid_hbm) | copy-start | bytes 12582916
  83.5 1.0 %copy-start.1 = (f32[1024,128]{1,0:T(8,128)S(1)}, f32[1024,128]{1,0:T(8,128)}, u32[]{:S(2)}) copy-start(f32[1024,128]{1,0:T(8,128)} %get-tuple-element.8.rows_ref) | copy-start | bytes 1572868
  84.5 1.0 %copy-start.2 = (f32[1024,128]{1,0:T(8,128)S(1)}, f32[1024,128]{1,0:T(8,128)}, u32[]{:S(2)}) copy-start(f32[1024,128]{1,0:T(8,128)} %get-tuple-element.9.heat_hbm) | copy-start | bytes 1572868

commit v2 on v1

v2 whole, which is shorter than its diff:
```python
import functools

import jax
import jax.numpy as jnp
from jax import lax
from jax.experimental import pallas as pl
from jax.experimental.pallas import tpu as pltpu
from jax.sharding import PartitionSpec as P

MESH = pl.DeviceIdType.MESH
F32 = jnp.float32
BF16 = jnp.bfloat16

NX, NY, NZ = 128, 64, 128
CELLS = NX * NY
GROUPS, CAP = 128, 8
SLOTS = GROUPS * CAP
HALF = 64

HOPS = (0, 1, 2, 1)
OFFSETS = sorted(
    [(a, b, c, d) for a in range(4) for b in range(4) for c in range(4) for d in range(2)][1:],
    key=lambda o: -(HOPS[o[0]] + HOPS[o[1]] + HOPS[o[2]] + 0.3 * o[3]),
)


def iota(shape, dim):
    return lax.broadcasted_iota(jnp.int32, shape, dim)


def dot(a, b):
    return jnp.dot(a, b, preferred_element_type=F32)


def parts_of(x):
    hi = x.astype(BF16)
    return hi, (x - hi.astype(F32)).astype(BF16)


def one_hot(mask):
    return jnp.where(mask, 1.0, 0.0).astype(BF16)


def tall(row):
    eye = iota((128, 128), 0) == iota((128, 128), 1)
    spread = jnp.where(eye, row.astype(F32), 0.0).astype(BF16)
    return dot(spread, jnp.ones((128, 128), BF16))


def rate_of(c, xm, xp, ym, yp, flux, mix):
    vx, vy, vz = flux
    kh, kv = mix
    lane = iota(c.shape, 1)
    zm = jnp.where(lane == 0, 0.0, pltpu.roll(c, 1, 1))
    zp = jnp.where(lane == NZ - 1, 0.0, pltpu.roll(c, NZ - 1, 1))
    xa, xb, ya, yb, za, zb = xp - c, c - xm, yp - c, c - ym, zp - c, c - zm
    advect = vx * jnp.where(vx > 0.0, xb, xa)
    advect += vy * jnp.where(vy > 0.0, yb, ya)
    advect += vz * jnp.where(vz > 0.0, zb, za)
    return c + 0.1 * (kh * ((xa - xb) + (ya - yb)) + kv * (za - zb) - advect)


def transport(
    site,
    u_hbm,
    flux_hbm,
    mix_hbm,
    first_ref,
    stop_ref,
    site_ref,
    lookup_row,
    solver_hbm,
    grid_out,
    columns_out,
    heat_out,
    state,
    after,
    flux,
    mix,
    xhalo,
    yhalo,
    yface,
    base,
    masks,
    pack_own,
    unpack_own,
    pack_got,
    unpack_got,
    lookup_mat,
    return_mat,
    cell_mat,
    solver,
    blocks,
    rhs,
    heat,
    row_hot,
    pick_a,
    pick_b,
    out_box,
    in_box,
    out_one,
    in_one,
    load_sem,
    store_sem,
    halo_send,
    halo_recv,
    send_sem,
    recv_sem,
):
    gx, gy = lax.axis_index("gx"), lax.axis_index("gy")
    me = gx * 8 + gy
    px, py = lax.div(gx, 4), lax.rem(gx, 4)
    pz, pc = lax.div(gy, 2), lax.rem(gy, 2)
    xs = [lax.rem(px + i, 4) for i in range(4)]
    ys = [lax.rem(py + i, 4) for i in range(4)]
    zs = [lax.rem(pz + i, 4) for i in range(4)]
    cs = [lax.rem(pc + i, 2) for i in range(2)]
    peers = [(xs[a] * 4 + ys[b], zs[c] * 2 + cs[d]) for a, b, c, d in OFFSETS]

    loads = [
        pltpu.make_async_copy(source, target, load_sem.at[i])
        for i, (source, target) in enumerate(
            ((u_hbm, state), (flux_hbm, flux), (mix_hbm, mix), (solver_hbm, solver))
        )
    ]
    for load in loads:
        load.start()
    barrier = pltpu.get_barrier_semaphore()
    for peer in peers:
        pl.semaphore_signal(barrier, inc=1, device_id=peer, device_id_type=MESH)

    lane = iota((128, 128), 1)

    def block(c):
        return slice(c * 128, c * 128 + 128)

    def indices(c, first, pack_ref, unpack_ref):
        shift = HALF if c >= 4 else 0
        pack_ref[block(c), :] = (lane + first + shift) & 127
        unpack_ref[block(c), :] = (lane - first + shift) & 127

    def pack(value, index, box):
        for r in range(4):
            left, right = (
                jnp.take_along_axis(value(c), index[block(c), :], axis=1) for c in (r, r + 4)
            )
            box[:, r, :] = jnp.where(lane < HALF, left, right)

    def unpack(box, index, keep):
        for r in range(4):
            pair = box[:, r, :]
            for c in (r, r + 4):
                wide = jnp.take_along_axis(pair, index[block(c), :], axis=1)
                hi, lo = parts_of(jnp.where(keep(c), wide, 0.0))
                rhs[block(c), 0:128] = hi
                rhs[block(c), 128:256] = lo

    def own(c):
        return masks[block(c), :] > 0.0

    def got(c):
        return ((unpack_got[block(c), :] - (HALF if c >= 4 else 0)) & 127) < HALF

    def send(box, landing, k):
        for x, y in peers:
            pltpu.make_async_remote_copy(
                box.at[x * 8 + y],
                landing.at[me],
                send_sem.at[k],
                recv_sem.at[k],
                device_id=(x, y),
                device_id_type=MESH,
            ).start()
        landing[me] = box[me]

    def receive(landing, k):
        some = landing.at[pl.ds(0, GROUPS - 1)]
        pltpu.make_async_copy(some, some, recv_sem.at[k]).wait()

    def sent(box, k):
        some = box.at[pl.ds(0, GROUPS - 1)]
        pltpu.make_async_copy(some, some, send_sem.at[k]).wait()

    def halo_copies(step):
        low_x, high_x = state.at[pl.ds(0, NY)], state.at[pl.ds(CELLS - NY, NY)]
        low_y, high_y = yface.at[step, 0], yface.at[step, 1]
        plan = [
            (gx > 0, low_x, xhalo.at[step, 1], 1, (gx - 1, gy)),
            (gx < 15, high_x, xhalo.at[step, 0], 0, (gx + 1, gy)),
            (gy > 0, low_y, yhalo.at[step, 1], 3, (gx, gy - 1)),
            (gy < 7, high_y, yhalo.at[step, 0], 2, (gx, gy + 1)),
        ]
        return [
            (
                there,
                pltpu.make_async_remote_copy(
                    source,
                    target,
                    halo_send.at[step, side],
                    halo_recv.at[step, side],
                    device_id=device,
                    device_id_type=MESH,
                ),
            )
            for there, source, target, side, device in plan
        ]

    def halo_faces(step):
        def face(i, carry):
            yface[step, 0, pl.ds(i, 1), :] = state[pl.ds(i * NY, 1), :]
            yface[step, 1, pl.ds(i, 1), :] = state[pl.ds(i * NY + NY - 1, 1), :]
            return carry

        lax.fori_loop(0, NX, face, 0, unroll=8)

    def halo_start(step):
        for there, copy in halo_copies(step):

            @pl.when(there)
            def _():
                copy.start()

    def halo_wait(step):
        for there, copy in halo_copies(step):

            @pl.when(there)
            def _():
                copy.wait_send()

        for there, side in ((gx > 0, 0), (gx < 15, 1), (gy > 0, 2), (gy < 7, 3)):
            halo = xhalo.at[step, side] if side < 2 else yhalo.at[step, side - 2]

            @pl.when(there)
            def _():
                pltpu.make_async_copy(halo, halo, halo_recv.at[step, side]).wait()

    def stencil(step, start, stop):
        size = 16
        row = iota((size, NZ), 0)
        last = NY // size - 1

        def slab(i, below, above):
            for b in range(last + 1):
                o = pl.multiple_of(i * NY + b * size, size)
                here = pl.ds(o, size)
                c = state[here, :]
                if b > 0:
                    ym = state[pl.ds(o - 1, size), :]
                else:
                    ym = jnp.where(row == 0, yhalo[step, 0, pl.ds(i, 1), :], pltpu.roll(c, 1, 0))
                if b < last:
                    yp = state[pl.ds(o + 1, size), :]
                else:
                    edge = yhalo[step, 1, pl.ds(i, 1), :]
                    yp = jnp.where(row == size - 1, edge, pltpu.roll(c, size - 1, 0))
                after[here, :] = rate_of(
                    c,
                    below(b * size, size),
                    above(b * size, size),
                    ym,
                    yp,
                    [flux[d, here, :].astype(F32) for d in range(3)],
                    [mix[d, here, :].astype(F32) for d in range(2)],
                )

        def at(i):
            return lambda r, n: state[pl.ds(pl.multiple_of(i * NY + r, 16), n), :]

        def halo(side):
            return lambda r, n: xhalo[step, side, r : r + n, :]

        def inner(i, carry):
            slab(i, at(i - 1), at(i + 1))
            return carry

        if start == 0:
            slab(0, halo(0), at(1))
        lax.fori_loop(max(start, 1), min(stop, NX - 1), inner, 0, unroll=7)
        if stop == NX:
            slab(NX - 1, at(NX - 2), halo(1))

    def gather(source, target):
        def group(o, carry):
            for c in range(CAP):
                target[pl.ds(c * 128 + o, 1), :] = source[pl.ds(site[c, o], 1), :]
            return carry

        lax.fori_loop(0, GROUPS, group, 0, unroll=4)

    def solve(last):
        loops = dot(lookup_mat[...], rhs[...]).astype(BF16)
        for g in range(4):
            rows = slice(g * 256, g * 256 + 256)
            two = dot(blocks[0, rows, :], loops[rows])
            small = dot(blocks[1, rows, :], loops[rows, 0:128])
            rates = two[:, 0:128] + two[:, 128:256] + small
            if last:
                heat[rows, :] = rates
            hi, lo = parts_of(rates)
            rhs[rows, 0:128] = hi
            rhs[rows, 128:256] = lo

    def product(matrix):
        two = dot(matrix[...], rhs[...])
        return lambda c: two[block(c), 0:128] + two[block(c), 128:256]

    for edge, halo, side in ((gx == 0, xhalo, 0), (gx == 15, xhalo, 1), (gy == 0, yhalo, 0), (gy == 7, yhalo, 1)):

        @pl.when(edge)
        def _():
            halo[:, side] = jnp.zeros_like(halo[:, side])

    table = jnp.zeros((128, 128), F32)
    for c in range(CAP):
        first, stop = tall(first_ref[c : c + 1, :]), tall(stop_ref[c : c + 1, :])
        table = jnp.where(lane == c, first, table)
        first, stop = first.astype(jnp.int32), stop.astype(jnp.int32)
        masks[block(c), :] = jnp.where((lane >= first) & (lane < stop), 1.0, 0.0)
        indices(c, first, pack_own, unpack_own)
    out_one[:, 4, :] = table
    loads[0].wait()
    gather(state, base)
    pack(lambda c: base[block(c), :] * masks[block(c), :], pack_own, out_one)
    halo_faces(0)

    lookup = lookup_row[...]
    lookup = jnp.where(lookup < SLOTS, (lookup & 7) * 128 + lax.shift_right_logical(lookup, 3), SLOTS)

    def build(o, carry):
        rows = pl.ds(pl.multiple_of(o * 128, 128), 128)
        return_mat[rows, :] = one_hot(lookup == iota((128, SLOTS), 0) + o * 128)
        return carry

    lax.fori_loop(0, 8, build, 0)
    pl.semaphore_wait(barrier, GROUPS - 1)
    halo_start(0)
    send(out_one, in_one, 0)

    for o in range(8):
        piece = lookup[:, block(o)]
        column = (tall(lax.shift_right_logical(piece, 3)) * 8.0 + tall(piece & 7)).astype(jnp.int32)
        for c in range(CAP):
            lookup_mat[block(o), block(c)] = one_hot(column == lane + c * 128)
    loads[3].wait()
    tile = one_hot(iota((32, 256), 1) % 32 == iota((32, 256), 0))
    own_block = (iota((SLOTS, 256), 0) // 32) % 8 == iota((SLOTS, 256), 1) // 32
    for part, piece in enumerate(parts_of(solver[...])):
        blocks[part] = jnp.where(own_block, dot(piece, tile), 0.0).astype(BF16)

    loads[1].wait()
    loads[2].wait()
    halo_wait(0)
    stencil(0, 0, 64)
    receive(in_one, 0)
    sources = in_one[:, 4, :]
    for c in range(CAP):
        first = dot(jnp.where(lane == c, sources, 0.0).astype(BF16), jnp.ones((128, 128), BF16))
        indices(c, first.astype(jnp.int32), pack_got, unpack_got)
    unpack(in_one, unpack_got, got)
    solve(False)
    pack(product(return_mat), pack_got, out_box.at[0])
    send(out_box.at[0], in_box.at[0], 1)

    stencil(0, 64, 128)
    gather(after, base)
    for o in range(CAP):
        piece = site_ref[o : o + 1, :]
        column = (tall(lax.shift_right_logical(piece, 6)) * 64.0 + tall(piece & 63)).astype(jnp.int32)
        for q in range(CAP):
            cell_mat[block(o), block(q)] = one_hot(column == site_ref[q : q + 1, :])
    for q in range(CAP):
        row_hot[:, block(q)] = one_hot((site_ref[q : q + 1, :] & 63) == iota((NY, 128), 0))

    receive(in_box.at[0], 1)
    unpack(in_box.at[0], unpack_own, own)
    deposit = product(cell_mat)
    pack(lambda c: (base[block(c), :] - deposit(c)) * masks[block(c), :], pack_own, out_box.at[1])
    send(out_box.at[1], in_box.at[1], 2)

    def picks(o, target):
        for i in range(16):
            for q in range(CAP):
                there = lax.shift_right_logical(site_ref[q : q + 1, :], 6) == o * 16 + i
                there = one_hot(jnp.broadcast_to(there, (16, 128)))
                for r in range(NY // 16):
                    rows = slice(r * 16, r * 16 + 16)
                    target[i * NY + r * 16 : i * NY + r * 16 + 16, block(q)] = row_hot[rows, block(q)] * there

    def lay(o, source):
        rows = pl.ds(pl.multiple_of(o * 1024, 1024), 1024)
        two = dot(source[...], rhs[...])
        state[rows, :] = after[rows, :] - (two[:, 0:128] + two[:, 128:256])

    def two_blocks(o, carry):
        picks(2 * o + 1, pick_b)
        lay(2 * o, pick_a)
        picks(2 * o + 2, pick_a)
        lay(2 * o + 1, pick_b)
        return carry

    picks(0, pick_a)
    lax.fori_loop(0, 4, two_blocks, 0)
    halo_faces(1)
    halo_start(1)
    receive(in_box.at[1], 2)
    unpack(in_box.at[1], unpack_got, got)
    solve(True)
    pack(product(return_mat), pack_got, out_box.at[2])
    send(out_box.at[2], in_box.at[2], 3)
    store_heat = pltpu.make_async_copy(heat, heat_out, store_sem.at[1])
    store_heat.start()

    halo_wait(1)
    stencil(1, 0, 128)
    store = pltpu.make_async_copy(after, grid_out, store_sem.at[0])
    store.start()
    gather(after, base)
    receive(in_box.at[2], 3)
    unpack(in_box.at[2], unpack_own, own)
    deposit = product(cell_mat)
    for c in range(CAP):
        columns_out[block(c), :] = base[block(c), :] - deposit(c)
    sent(out_one, 0)
    for k in range(3):
        sent(out_box.at[k], k + 1)
    store_heat.wait()
    store.wait()


def settle(site, grid_hbm, rows_hbm, heat_hbm, out_hbm, heat_out, held, rows_ref, heat_ref, sem):
    load = pltpu.make_async_copy(grid_hbm, held, sem.at[0])
    rows = pltpu.make_async_copy(rows_hbm, rows_ref, sem.at[1])
    heat = pltpu.make_async_copy(heat_hbm, heat_ref, sem.at[2])
    load.start()
    rows.start()
    heat.start()
    heat.wait()
    heat = pltpu.make_async_copy(heat_ref, heat_out, sem.at[2])
    heat.start()
    rows.wait()
    load.wait()

    def group(o, carry):
        for c in range(CAP):
            held[pl.ds(site[c, o], 1), :] = rows_ref[pl.ds(c * 128 + o, 1), :]
        return carry

    lax.fori_loop(0, GROUPS, group, 0, unroll=4)
    store = pltpu.make_async_copy(held, out_hbm, sem.at[3])
    store.start()
    store.wait()
    heat.wait()


VMEM = pl.BlockSpec(memory_space=pltpu.VMEM)
SMEM = pl.BlockSpec(memory_space=pltpu.SMEM)
ANY = pl.BlockSpec(memory_space=pl.ANY)


def local(u, flux, mix, site, first, stop, lookup, order, solver):
    def flat(table):
        return jnp.swapaxes(table.reshape(GROUPS, CAP), 0, 1)

    slots = flat(site)
    grid_shape = jax.ShapeDtypeStruct((CELLS, NZ), F32)
    slot_shape = jax.ShapeDtypeStruct((SLOTS, NZ), F32)
    slot_f32 = pltpu.VMEM((SLOTS, NZ), F32)
    slot_i32 = pltpu.VMEM((SLOTS, NZ), jnp.int32)
    square = pltpu.VMEM((SLOTS, SLOTS), BF16)
    grid, rows, heat = pl.pallas_call(
        transport,
        out_shape=(grid_shape, slot_shape, slot_shape),
        in_specs=[SMEM, ANY, ANY, ANY] + [VMEM] * 4 + [ANY],
        out_specs=(ANY, VMEM, ANY),
        scratch_shapes=[
            pltpu.VMEM((CELLS, NZ), F32),
            pltpu.VMEM((CELLS, NZ), F32),
            pltpu.VMEM((3, CELLS, NZ), BF16),
            pltpu.VMEM((2, CELLS, NZ), BF16),
            pltpu.VMEM((2, 2, NY, NZ), F32),
            pltpu.VMEM((2, 2, NX, NZ), F32),
            pltpu.VMEM((2, 2, NX, NZ), F32),
            slot_f32,
            slot_f32,
            slot_i32,
            slot_i32,
            slot_i32,
            slot_i32,
            square,
            square,
            square,
            pltpu.VMEM((SLOTS, 32), F32),
            pltpu.VMEM((2, SLOTS, 256), BF16),
            pltpu.VMEM((SLOTS, 256), BF16),
            slot_f32,
            pltpu.VMEM((NY, SLOTS), BF16),
            square,
            square,
            pltpu.VMEM((3, GROUPS, 4, NZ), F32),
            pltpu.VMEM((3, GROUPS, 4, NZ), F32),
            pltpu.VMEM((GROUPS, 5, NZ), F32),
            pltpu.VMEM((GROUPS, 5, NZ), F32),
            pltpu.SemaphoreType.DMA((4,)),
            pltpu.SemaphoreType.DMA((2,)),
            pltpu.SemaphoreType.DMA((2, 4)),
            pltpu.SemaphoreType.DMA((2, 4)),
            pltpu.SemaphoreType.DMA((4,)),
            pltpu.SemaphoreType.DMA((4,)),
        ],
        compiler_params=pltpu.CompilerParams(
            collective_id=0, has_side_effects=True, vmem_limit_bytes=60 << 20
        ),
    )(
        slots,
        u.reshape(CELLS, NZ),
        flux.reshape(3, CELLS, NZ),
        mix.reshape(2, CELLS, NZ),
        flat(first),
        flat(stop),
        slots,
        lookup.reshape(1, SLOTS),
        solver.reshape(SLOTS, 32),
    )
    grid, heat = pl.pallas_call(
        settle,
        out_shape=(grid_shape, slot_shape),
        in_specs=[SMEM, ANY, ANY, ANY],
        out_specs=(ANY, ANY),
        scratch_shapes=[pltpu.VMEM((CELLS, NZ), F32), slot_f32, slot_f32, pltpu.SemaphoreType.DMA((4,))],
        compiler_params=pltpu.CompilerParams(vmem_limit_bytes=60 << 20),
    )(slots, grid, rows, heat)
    return grid.reshape(NX, NY, NZ), heat.reshape(1, 1, SLOTS, NZ)


def solution(mesh):
    placed = (
        P("gx", "gy", None),
        P(None, "gx", "gy", None),
        P(None, "gx", "gy", None),
        P("gx", "gy", None, None),
        P("gx", "gy", None, None),
        P("gx", "gy", None, None),
        P("gx", "gy", None),
        P("gx", "gy", None),
        P("gx", "gy", None, None, None),
    )
    return jax.shard_map(
        local,
        mesh=mesh,
        in_specs=placed,
        out_specs=(P("gx", "gy", None), P("gx", "gy", None, None)),
        check_vma=False,
    )
```

time: 89.8 us -> 58.6 us (0.65)
  Pallas kernels: 79.6 us -> 57.6 us
  local copies, waits for them, and re-layouts: 9.25 us -> 0 us
    pallas_call x1, Pallas kernels: 75.7 us -> 50.9 us  [local(): pl.pallas_call(transport, out_shape=(grid_shape, slot_shape, slot_shape),...]
    unnamed x11 -> x0, local copies, waits for them, and re-layouts: 7.88 us -> none
    pallas_call x1, Pallas kernels: 3.91 us -> 6.73 us  [local(): pl.pallas_call(settle, out_shape=(grid_shape, slot_shape), in_specs=[SMEM...]
where the time goes in v2:
time: 58.6 us; the launch traced here: 58.4 us
  Pallas kernels  57.6 us (98%)
  between operations  0.8 us (1%)
    pallas_call x1, Pallas kernels, local(): pl.pallas_call(transport, out_shape=(grid_shape, slot_shape, slot_shape),...  50.9 us
    pallas_call x1, Pallas kernels, local(): pl.pallas_call(settle, out_shape=(grid_shape, slot_shape), in_specs=[SMEM...  6.73 us

profile of v2, /device:TPU:1, one launch (start us, length us, event | category | flops | bytes accessed | tf_op | source)
XLA Modules:
  0.0 58.4 jit_solution(6240124049465074856)
XLA Ops:
  0.6 50.9 %shard_map.95 = (f32[8192,128]{1,0:T(8,128)}, f32[1024,128]{1,0:T(8,128)}, f32[1024,128]{1,0:T(8,128)}) custom-call(s32[8,128]{1,0:T(8,128)} %bitcast.20, f32[8192,128]{1,0:T(8,128)} %bitcast.17, bf16[3,8192,128]{2,1,0:T(8,128)(2,1)} %bitcast.16, bf16[2,8192,128]{2,1,0:T(8,128)(2,1)} %bitcast.18, s32[8,128]{1,0:T(8,128)} %bitcast.23, s32[8,128]{1,0:T(8,128)} %bitcast.24, ...), custom_call_target="tpu_custom_call" | custom-call | tf_op jit(solution)/shard_map/pallas_call | solution.py:470
  51.5 6.7 %shard_map.96 = (f32[8192,128]{1,0:T(8,128)}, f32[1024,128]{1,0:T(8,128)}) custom-call(s32[8,128]{1,0:T(8,128)} %bitcast.22, f32[8192,128]{1,0:T(8,128)} %get-tuple-element.7.grid_hbm, f32[1024,128]{1,0:T(8,128)} %get-tuple-element.8.rows_hbm, f32[1024,128]{1,0:T(8,128)} %get-tuple-element.9.heat_hbm), custom_call_target="tpu_custom_call" | custom-call | tf_op jit(solution)/shard_map/pallas_call | solution.py:524

commit v3 on v2

--- a/solution.py
+++ b/solution.py
@@ -61,20 +61,23 @@
 
 
 def transport(
-    site,
     u_hbm,
     flux_hbm,
     mix_hbm,
+    first_hbm,
+    stop_hbm,
+    site_hbm,
+    lookup_hbm,
+    solver_hbm,
+    after,
+    columns_out,
+    heat,
+    site,
     first_ref,
     stop_ref,
     site_ref,
     lookup_row,
-    solver_hbm,
-    grid_out,
-    columns_out,
-    heat_out,
     state,
-    after,
     flux,
     mix,
     xhalo,
@@ -92,7 +95,6 @@
     solver,
     blocks,
     rhs,
-    heat,
     row_hot,
     pick_a,
     pick_b,
@@ -101,7 +103,6 @@
     out_one,
     in_one,
     load_sem,
-    store_sem,
     halo_send,
     halo_recv,
     send_sem,
@@ -117,11 +118,20 @@
     cs = [lax.rem(pc + i, 2) for i in range(2)]
     peers = [(xs[a] * 4 + ys[b], zs[c] * 2 + cs[d]) for a, b, c, d in OFFSETS]
 
+    moves = (
+        (first_hbm, first_ref),
+        (stop_hbm, stop_ref),
+        (site_hbm, site),
+        (u_hbm, state),
+        (site_hbm, site_ref),
+        (lookup_hbm, lookup_row),
+        (solver_hbm, solver),
+        (flux_hbm, flux),
+        (mix_hbm, mix),
+    )
     loads = [
         pltpu.make_async_copy(source, target, load_sem.at[i])
-        for i, (source, target) in enumerate(
-            ((u_hbm, state), (flux_hbm, flux), (mix_hbm, mix), (solver_hbm, solver))
-        )
+        for i, (source, target) in enumerate(moves)
     ]
     for load in loads:
         load.start()
@@ -310,6 +320,8 @@
         def _():
             halo[:, side] = jnp.zeros_like(halo[:, side])
 
+    loads[0].wait()
+    loads[1].wait()
     table = jnp.zeros((128, 128), F32)
     for c in range(CAP):
         first, stop = tall(first_ref[c : c + 1, :]), tall(stop_ref[c : c + 1, :])
@@ -318,11 +330,13 @@
         masks[block(c), :] = jnp.where((lane >= first) & (lane < stop), 1.0, 0.0)
         indices(c, first, pack_own, unpack_own)
     out_one[:, 4, :] = table
-    loads[0].wait()
+    loads[2].wait()
+    loads[3].wait()
     gather(state, base)
     pack(lambda c: base[block(c), :] * masks[block(c), :], pack_own, out_one)
     halo_faces(0)
 
+    loads[5].wait()
     lookup = lookup_row[...]
     lookup = jnp.where(lookup < SLOTS, (lookup & 7) * 128 + lax.shift_right_logical(lookup, 3), SLOTS)
 
@@ -332,23 +346,23 @@
         return carry
 
     lax.fori_loop(0, 8, build, 0)
-    pl.semaphore_wait(barrier, GROUPS - 1)
-    halo_start(0)
-    send(out_one, in_one, 0)
-
     for o in range(8):
         piece = lookup[:, block(o)]
         column = (tall(lax.shift_right_logical(piece, 3)) * 8.0 + tall(piece & 7)).astype(jnp.int32)
         for c in range(CAP):
             lookup_mat[block(o), block(c)] = one_hot(column == lane + c * 128)
-    loads[3].wait()
+    loads[6].wait()
     tile = one_hot(iota((32, 256), 1) % 32 == iota((32, 256), 0))
     own_block = (iota((SLOTS, 256), 0) // 32) % 8 == iota((SLOTS, 256), 1) // 32
     for part, piece in enumerate(parts_of(solver[...])):
         blocks[part] = jnp.where(own_block, dot(piece, tile), 0.0).astype(BF16)
 
-    loads[1].wait()
-    loads[2].wait()
+    pl.semaphore_wait(barrier, GROUPS - 1)
+    halo_start(0)
+    send(out_one, in_one, 0)
+
+    for load in (loads[4], loads[7], loads[8]):
+        load.wait()
     halo_wait(0)
     stencil(0, 0, 64)
     receive(in_one, 0)
@@ -407,13 +421,9 @@
     solve(True)
     pack(product(return_mat), pack_got, out_box.at[2])
     send(out_box.at[2], in_box.at[2], 3)
-    store_heat = pltpu.make_async_copy(heat, heat_out, store_sem.at[1])
-    store_heat.start()
 
     halo_wait(1)
     stencil(1, 0, 128)
-    store = pltpu.make_async_copy(after, grid_out, store_sem.at[0])
-    store.start()
     gather(after, base)
     receive(in_box.at[2], 3)
     unpack(in_box.at[2], unpack_own, own)
@@ -423,38 +433,28 @@
     sent(out_one, 0)
     for k in range(3):
         sent(out_box.at[k], k + 1)
+
+
+def settle(site, grid, rows, heat, out_hbm, heat_out, changed, sem):
+    store_heat = pltpu.make_async_copy(heat, heat_out, sem.at[0])
+    store_heat.start()
+
+    def group(o, carry):
+        for c in range(CAP):
+            changed[pl.ds(site[c, o], 1), :] = rows[pl.ds(c * 128 + o, 1), :]
+        return carry
+
+    lax.fori_loop(0, GROUPS, group, 0, unroll=4)
+    store = pltpu.make_async_copy(changed, out_hbm, sem.at[1])
+    store.start()
     store_heat.wait()
     store.wait()
-
-
-def settle(site, grid_hbm, rows_hbm, heat_hbm, out_hbm, heat_out, held, rows_ref, heat_ref, sem):
-    load = pltpu.make_async_copy(grid_hbm, held, sem.at[0])
-    rows = pltpu.make_async_copy(rows_hbm, rows_ref, sem.at[1])
-    heat = pltpu.make_async_copy(heat_hbm, heat_ref, sem.at[2])
-    load.start()
-    rows.start()
-    heat.start()
-    heat.wait()
-    heat = pltpu.make_async_copy(heat_ref, heat_out, sem.at[2])
-    heat.start()
-    rows.wait()
-    load.wait()
-
-    def group(o, carry):
-        for c in range(CAP):
-            held[pl.ds(site[c, o], 1), :] = rows_ref[pl.ds(c * 128 + o, 1), :]
-        return carry
-
-    lax.fori_loop(0, GROUPS, group, 0, unroll=4)
-    store = pltpu.make_async_copy(held, out_hbm, sem.at[3])
-    store.start()
-    store.wait()
-    heat.wait()
 
 
 VMEM = pl.BlockSpec(memory_space=pltpu.VMEM)
 SMEM = pl.BlockSpec(memory_space=pltpu.SMEM)
 ANY = pl.BlockSpec(memory_space=pl.ANY)
+HBM = pl.BlockSpec(memory_space=pltpu.HBM)
 
 
 def local(u, flux, mix, site, first, stop, lookup, order, solver):
@@ -469,11 +469,15 @@
     square = pltpu.VMEM((SLOTS, SLOTS), BF16)
     grid, rows, heat = pl.pallas_call(
         transport,
-        out_shape=(grid_shape, slot_shape, slot_shape),
-        in_specs=[SMEM, ANY, ANY, ANY] + [VMEM] * 4 + [ANY],
-        out_specs=(ANY, VMEM, ANY),
+        out_shape=(pltpu.VMEM((CELLS, NZ), F32), pltpu.VMEM((SLOTS, NZ), F32), pltpu.VMEM((SLOTS, NZ), F32)),
+        in_specs=[HBM] * 8,
+        out_specs=(VMEM, VMEM, VMEM),
         scratch_shapes=[
-            pltpu.VMEM((CELLS, NZ), F32),
+            pltpu.SMEM((CAP, GROUPS), jnp.int32),
+            pltpu.VMEM((CAP, GROUPS), jnp.int32),
+            pltpu.VMEM((CAP, GROUPS), jnp.int32),
+            pltpu.VMEM((CAP, GROUPS), jnp.int32),
+            pltpu.VMEM((1, SLOTS), jnp.int32),
             pltpu.VMEM((CELLS, NZ), F32),
             pltpu.VMEM((3, CELLS, NZ), BF16),
             pltpu.VMEM((2, CELLS, NZ), BF16),
@@ -492,7 +496,6 @@
             pltpu.VMEM((SLOTS, 32), F32),
             pltpu.VMEM((2, SLOTS, 256), BF16),
             pltpu.VMEM((SLOTS, 256), BF16),
-            slot_f32,
             pltpu.VMEM((NY, SLOTS), BF16),
             square,
             square,
@@ -500,18 +503,16 @@
             pltpu.VMEM((3, GROUPS, 4, NZ), F32),
             pltpu.VMEM((GROUPS, 5, NZ), F32),
             pltpu.VMEM((GROUPS, 5, NZ), F32),
-            pltpu.SemaphoreType.DMA((4,)),
-            pltpu.SemaphoreType.DMA((2,)),
+            pltpu.SemaphoreType.DMA((9,)),
             pltpu.SemaphoreType.DMA((2, 4)),
             pltpu.SemaphoreType.DMA((2, 4)),
             pltpu.SemaphoreType.DMA((4,)),
             pltpu.SemaphoreType.DMA((4,)),
         ],
         compiler_params=pltpu.CompilerParams(
-            collective_id=0, has_side_effects=True, vmem_limit_bytes=60 << 20
+            collective_id=0, has_side_effects=True, vmem_limit_bytes=57 << 20
         ),
     )(
-        slots,
         u.reshape(CELLS, NZ),
         flux.reshape(3, CELLS, NZ),
         mix.reshape(2, CELLS, NZ),
@@ -521,13 +522,14 @@
         lookup.reshape(1, SLOTS),
         solver.reshape(SLOTS, 32),
     )
-    grid, heat = pl.pallas_call(
+    grid, heat, _ = pl.pallas_call(
         settle,
-        out_shape=(grid_shape, slot_shape),
-        in_specs=[SMEM, ANY, ANY, ANY],
-        out_specs=(ANY, ANY),
-        scratch_shapes=[pltpu.VMEM((CELLS, NZ), F32), slot_f32, slot_f32, pltpu.SemaphoreType.DMA((4,))],
-        compiler_params=pltpu.CompilerParams(vmem_limit_bytes=60 << 20),
+        out_shape=(grid_shape, slot_shape, pltpu.VMEM((CELLS, NZ), F32)),
+        in_specs=[SMEM, VMEM, VMEM, VMEM],
+        out_specs=(ANY, ANY, VMEM),
+        scratch_shapes=[pltpu.SemaphoreType.DMA((2,))],
+        input_output_aliases={1: 2},
+        compiler_params=pltpu.CompilerParams(vmem_limit_bytes=16 << 20),
     )(slots, grid, rows, heat)
     return grid.reshape(NX, NY, NZ), heat.reshape(1, 1, SLOTS, NZ)
 

time: 58.6 us -> 55.5 us (0.947)
  Pallas kernels: 57.6 us -> 54.6 us
    pallas_call x2, Pallas kernels: 57.6 us -> 54.6 us  [the longest x1 50.4 us: local(): pl.pallas_call(transport, out_shape=(pltpu.VMEM((CELLS, NZ), F32), pltpu....]
where the time goes in v3:
time: 55.5 us; the launch traced here: 55.4 us
  Pallas kernels  54.6 us (98%)
  between operations  0.82 us (1%)
    pallas_call x1, Pallas kernels, local(): pl.pallas_call(transport, out_shape=(pltpu.VMEM((CELLS, NZ), F32), pltpu....  50.4 us
    pallas_call x1, Pallas kernels, local(): pl.pallas_call(settle, out_shape=(grid_shape, slot_shape, pltpu.VMEM((CEL...  4.2 us

profile of v3, /device:TPU:1, one launch (start us, length us, event | category | flops | bytes accessed | tf_op | source)
XLA Modules:
  0.0 55.4 jit_solution(5339881689777332198)
XLA Ops:
  0.6 0.0 copy-start
  0.6 50.4 %shard_map.95 = (f32[8192,128]{1,0:T(8,128)S(1)}, f32[1024,128]{1,0:T(8,128)S(1)}, f32[1024,128]{1,0:T(8,128)S(1)}) custom-call(f32[8192,128]{1,0:T(8,128)} %bitcast.19, bf16[3,8192,128]{2,1,0:T(8,128)(2,1)} %bitcast.18, bf16[2,8192,128]{2,1,0:T(8,128)(2,1)} %bitcast.20, s32[8,128]{1,0:T(8,128)} %bitcast.22, s32[8,128]{1,0:T(8,128)} %bitcast.23, ...), custom_call_target="tpu_custom_call" | custom-call | tf_op jit(solution)/shard_map/pallas_call | solution.py:470
  51.0 0.0 copy-done
  51.1 4.2 %shard_map.96 = (f32[8192,128]{1,0:T(8,128)}, f32[1024,128]{1,0:T(8,128)}, f32[8192,128]{1,0:T(8,128)S(1)}) custom-call(s32[8,128]{1,0:T(8,128)S(1)} %bitcast.17, f32[8192,128]{1,0:T(8,128)S(1)} %get-tuple-element.7.grid, f32[1024,128]{1,0:T(8,128)S(1)} %get-tuple-element.8.rows, f32[1024,128]{1,0:T(8,128)S(1)} %get-tuple-element.9.heat), custom_call_target="tpu_custom_call", output_to_operand_aliasing={{2}: (1, {})} | custom-call | tf_op jit(solution)/shard_map/pallas_call | solution.py:525
Async XLA Ops:
  0.6 50.4 %copy-start = (s32[1,1,128,8]{2,3,1,0:T(8,128)S(1)}, s32[1,1,128,8]{2,3,1,0:T(8,128)}, u32[]{:S(2)}) copy-start(s32[1,1,128,8]{2,3,1,0:T(8,128)} %param.12) | copy-start | bytes 12292

commit v4 on v3

--- a/solution.py
+++ b/solution.py
@@ -147,7 +147,8 @@
     def indices(c, first, pack_ref, unpack_ref):
         shift = HALF if c >= 4 else 0
         pack_ref[block(c), :] = (lane + first + shift) & 127
-        unpack_ref[block(c), :] = (lane - first + shift) & 127
+        if unpack_ref is not None:
+            unpack_ref[block(c), :] = (lane - first + shift) & 127
 
     def pack(value, index, box):
         for r in range(4):
@@ -328,13 +329,20 @@
         table = jnp.where(lane == c, first, table)
         first, stop = first.astype(jnp.int32), stop.astype(jnp.int32)
         masks[block(c), :] = jnp.where((lane >= first) & (lane < stop), 1.0, 0.0)
-        indices(c, first, pack_own, unpack_own)
+        indices(c, first, pack_own, None)
     out_one[:, 4, :] = table
     loads[2].wait()
     loads[3].wait()
     gather(state, base)
     pack(lambda c: base[block(c), :] * masks[block(c), :], pack_own, out_one)
     halo_faces(0)
+
+    pl.semaphore_wait(barrier, GROUPS - 1)
+    halo_start(0)
+    send(out_one, in_one, 0)
+
+    for c in range(CAP):
+        unpack_own[block(c), :] = (2 * lane - pack_own[block(c), :]) & 127
 
     loads[5].wait()
     lookup = lookup_row[...]
@@ -356,10 +364,6 @@
     own_block = (iota((SLOTS, 256), 0) // 32) % 8 == iota((SLOTS, 256), 1) // 32
     for part, piece in enumerate(parts_of(solver[...])):
         blocks[part] = jnp.where(own_block, dot(piece, tile), 0.0).astype(BF16)
-
-    pl.semaphore_wait(barrier, GROUPS - 1)
-    halo_start(0)
-    send(out_one, in_one, 0)
 
     for load in (loads[4], loads[7], loads[8]):
         load.wait()

time: 55.5 us -> 54.2 us (0.977)
  Pallas kernels: 54.6 us -> 53.3 us
    pallas_call x1, Pallas kernels: 50.4 us -> 49.1 us  [local(): pl.pallas_call(transport, out_shape=(pltpu.VMEM((CELLS, NZ), F32), pltpu....]
where the time goes in v4:
time: 54.2 us; the launch traced here: 54.1 us
  Pallas kernels  53.3 us (98%)
  between operations  0.82 us (2%)
    pallas_call x1, Pallas kernels, local(): pl.pallas_call(transport, out_shape=(pltpu.VMEM((CELLS, NZ), F32), pltpu....  49.1 us
    pallas_call x1, Pallas kernels, local(): pl.pallas_call(settle, out_shape=(grid_shape, slot_shape, pltpu.VMEM((CEL...  4.2 us

profile of v4, /device:TPU:1, one launch (start us, length us, event | category | flops | bytes accessed | tf_op | source)
XLA Modules:
  0.0 54.1 jit_solution(17802262849435399678)
XLA Ops:
  0.6 0.0 copy-start
  0.6 49.1 %shard_map.95 = (f32[8192,128]{1,0:T(8,128)S(1)}, f32[1024,128]{1,0:T(8,128)S(1)}, f32[1024,128]{1,0:T(8,128)S(1)}) custom-call(f32[8192,128]{1,0:T(8,128)} %bitcast.19, bf16[3,8192,128]{2,1,0:T(8,128)(2,1)} %bitcast.18, bf16[2,8192,128]{2,1,0:T(8,128)(2,1)} %bitcast.20, s32[8,128]{1,0:T(8,128)} %bitcast.22, s32[8,128]{1,0:T(8,128)} %bitcast.23, ...), custom_call_target="tpu_custom_call" | custom-call | tf_op jit(solution)/shard_map/pallas_call | solution.py:474
  49.7 0.0 copy-done
  49.8 4.2 %shard_map.96 = (f32[8192,128]{1,0:T(8,128)}, f32[1024,128]{1,0:T(8,128)}, f32[8192,128]{1,0:T(8,128)S(1)}) custom-call(s32[8,128]{1,0:T(8,128)S(1)} %bitcast.17, f32[8192,128]{1,0:T(8,128)S(1)} %get-tuple-element.7.grid, f32[1024,128]{1,0:T(8,128)S(1)} %get-tuple-element.8.rows, f32[1024,128]{1,0:T(8,128)S(1)} %get-tuple-element.9.heat), custom_call_target="tpu_custom_call", output_to_operand_aliasing={{2}: (1, {})} | custom-call | tf_op jit(solution)/shard_map/pallas_call | solution.py:529
Async XLA Ops:
  0.6 49.1 %copy-start = (s32[1,1,128,8]{2,3,1,0:T(8,128)S(1)}, s32[1,1,128,8]{2,3,1,0:T(8,128)}, u32[]{:S(2)}) copy-start(s32[1,1,128,8]{2,3,1,0:T(8,128)} %param.12) | copy-start | bytes 12292

commit v5 on v4

--- a/solution.py
+++ b/solution.py
@@ -315,12 +315,6 @@
         two = dot(matrix[...], rhs[...])
         return lambda c: two[block(c), 0:128] + two[block(c), 128:256]
 
-    for edge, halo, side in ((gx == 0, xhalo, 0), (gx == 15, xhalo, 1), (gy == 0, yhalo, 0), (gy == 7, yhalo, 1)):
-
-        @pl.when(edge)
-        def _():
-            halo[:, side] = jnp.zeros_like(halo[:, side])
-
     loads[0].wait()
     loads[1].wait()
     table = jnp.zeros((128, 128), F32)
@@ -335,11 +329,16 @@
     loads[3].wait()
     gather(state, base)
     pack(lambda c: base[block(c), :] * masks[block(c), :], pack_own, out_one)
+
+    pl.semaphore_wait(barrier, GROUPS - 1)
+    send(out_one, in_one, 0)
     halo_faces(0)
-
-    pl.semaphore_wait(barrier, GROUPS - 1)
     halo_start(0)
-    send(out_one, in_one, 0)
+    for edge, halo, side in ((gx == 0, xhalo, 0), (gx == 15, xhalo, 1), (gy == 0, yhalo, 0), (gy == 7, yhalo, 1)):
+
+        @pl.when(edge)
+        def _():
+            halo[:, side] = jnp.zeros_like(halo[:, side])
 
     for c in range(CAP):
         unpack_own[block(c), :] = (2 * lane - pack_own[block(c), :]) & 127
@@ -368,7 +367,7 @@
     for load in (loads[4], loads[7], loads[8]):
         load.wait()
     halo_wait(0)
-    stencil(0, 0, 64)
+    stencil(0, 0, 29)
     receive(in_one, 0)
     sources = in_one[:, 4, :]
     for c in range(CAP):
@@ -379,7 +378,7 @@
     pack(product(return_mat), pack_got, out_box.at[0])
     send(out_box.at[0], in_box.at[0], 1)
 
-    stencil(0, 64, 128)
+    stencil(0, 29, 128)
     gather(after, base)
     for o in range(CAP):
         piece = site_ref[o : o + 1, :]

time: 54.2 us -> 54.5 us (level)
  no operation moved by 1% of the time
where the time goes in v5:
time: 54.5 us; the launch traced here: 54.4 us
  Pallas kernels  53.6 us (98%)
  between operations  0.82 us (2%)
    pallas_call x1, Pallas kernels, local(): pl.pallas_call(transport, out_shape=(pltpu.VMEM((CELLS, NZ), F32), pltpu....  49.4 us
    pallas_call x1, Pallas kernels, local(): pl.pallas_call(settle, out_shape=(grid_shape, slot_shape, pltpu.VMEM((CEL...  4.2 us

profile of v5, /device:TPU:1, one launch (start us, length us, event | category | flops | bytes accessed | tf_op | source)
XLA Modules:
  0.0 54.4 jit_solution(2234635433215594661)
XLA Ops:
  0.6 0.0 copy-start
  0.6 49.4 %shard_map.95 = (f32[8192,128]{1,0:T(8,128)S(1)}, f32[1024,128]{1,0:T(8,128)S(1)}, f32[1024,128]{1,0:T(8,128)S(1)}) custom-call(f32[8192,128]{1,0:T(8,128)} %bitcast.19, bf16[3,8192,128]{2,1,0:T(8,128)(2,1)} %bitcast.18, bf16[2,8192,128]{2,1,0:T(8,128)(2,1)} %bitcast.20, s32[8,128]{1,0:T(8,128)} %bitcast.22, s32[8,128]{1,0:T(8,128)} %bitcast.23, ...), custom_call_target="tpu_custom_call" | custom-call | tf_op jit(solution)/shard_map/pallas_call | solution.py:473
  50.0 0.0 copy-done
  50.0 4.2 %shard_map.96 = (f32[8192,128]{1,0:T(8,128)}, f32[1024,128]{1,0:T(8,128)}, f32[8192,128]{1,0:T(8,128)S(1)}) custom-call(s32[8,128]{1,0:T(8,128)S(1)} %bitcast.17, f32[8192,128]{1,0:T(8,128)S(1)} %get-tuple-element.7.grid, f32[1024,128]{1,0:T(8,128)S(1)} %get-tuple-element.8.rows, f32[1024,128]{1,0:T(8,128)S(1)} %get-tuple-element.9.heat), custom_call_target="tpu_custom_call", output_to_operand_aliasing={{2}: (1, {})} | custom-call | tf_op jit(solution)/shard_map/pallas_call | solution.py:528
Async XLA Ops:
  0.6 49.4 %copy-start = (s32[1,1,128,8]{2,3,1,0:T(8,128)S(1)}, s32[1,1,128,8]{2,3,1,0:T(8,128)}, u32[]{:S(2)}) copy-start(s32[1,1,128,8]{2,3,1,0:T(8,128)} %param.12) | copy-start | bytes 12292
